TPU v7x, 32 devices: a whole 2x2x4 slice. The times are simulated.
32 devices in a mesh: dp: 4 (over z), tm: 8 (over y, x, core).
Axes of the slice: x: 2, y: 2, z: 4, core: 2. Of those that a mesh axis runs over, the one named last changes fastest.
Arguments:
- frames_in: bfloat16 [4, 24, 8, 8, 320], P('dp', 'tm'), may hold values from -6 to 6
- cotangent: bfloat16 [4, 24, 8, 8, 320], P('dp', 'tm'), may hold values from -6 to 6
- counts: int32 [4, 8], P('dp'), may hold values from 1 to 3, 16 in all within a row
- norm_gain: float32 [320], replicated, may hold values from 0.5 to 1.5
- norm_shift: float32 [320], replicated, may hold values from -3 to 3
- spatial_weight: bfloat16 [2880, 320], replicated, may hold values from -0.109375 to 0.109375
- temporal_weight: bfloat16 [960, 320], replicated, may hold values from -0.1875 to 0.1875
Outputs:
- input_grad: bfloat16 [4, 24, 8, 8, 320], P('dp', 'tm')
- temporal_grad: float32 [960, 320], replicated
Inputs may be any that keep to these rules, and one draw needn't show every extreme that they name: `counts`: each row sums to 16; in every row some index of tm holds exactly 3 frames.
All inputs are finite; a program needn't handle non-finite values.
Results may differ from a plain program's by a relative error of at most 0.006.
Values may be sent and summed in bfloat16 or wider, within the bound.
A program may use at most 64 MiB of HBM per device.

v0:
```python
import math

import jax
import jax.numpy as jnp
from jax import lax
from jax.sharding import PartitionSpec as P

GROUPS = 32


def norm_act(values, gain, shift, groups):
    nframes, height, width, channels = values.shape
    per_group = channels // groups
    entries = height * width * per_group

    def group_mean(totals):
        summed = totals.reshape(nframes, groups, per_group).sum(axis=2) / entries
        return jnp.repeat(summed, per_group, axis=1).reshape(nframes, 1, 1, channels)

    centre = group_mean(values.sum(axis=(1, 2)))
    centred = values - centre
    spread = group_mean((centred * centred).sum(axis=(1, 2)))
    normed = centred * lax.rsqrt(spread + 1e-05) * gain + shift
    return jax.nn.silu(normed)


def patches(field):
    height, width = (field.shape[1], field.shape[2])
    padded = jnp.pad(field, ((0, 0), (1, 1), (1, 1), (0, 0)))
    pieces = [
        padded[:, row_off : row_off + height, col_off : col_off + width, :]
        for row_off in range(3)
        for col_off in range(3)
    ]
    return jnp.concatenate(pieces, axis=3)


def spatial_conv(field, weight):
    stacked = patches(field)
    leading = stacked.shape[:3]
    product = jnp.dot(
        stacked.reshape(-1, stacked.shape[3]), weight, preferred_element_type=jnp.float32
    )
    return product.reshape(leading + (weight.shape[1],))


def spatial_conv_t(field, weight):
    channels = weight.shape[1]
    flipped = (
        weight.reshape(9, -1, channels)[::-1].transpose(0, 2, 1).reshape(-1, weight.shape[0] // 9)
    )
    return spatial_conv(field, flipped)


def silu_grad(values):
    sigma = jax.nn.sigmoid(values)
    return sigma * (1.0 + values * (1.0 - sigma))


def temporal_core(y_ext, g_ext, weight):
    nframes = y_ext.shape[0] - 2
    channels = weight.shape[1]
    units = jax.nn.silu(y_ext.astype(jnp.float32)).astype(jnp.bfloat16)
    g_middle = g_ext[1:-1]
    g_mid = g_middle.reshape(-1, channels)
    grads = []
    back_sum = jnp.zeros((g_mid.shape[0], channels), jnp.float32)
    for tap_k in range(3):
        taken = units[tap_k : tap_k + nframes].reshape(-1, channels)
        grads.append(
            lax.dot_general(
                taken, g_mid, (((0,), (0,)), ((), ())), preferred_element_type=jnp.float32
            )
        )
        tap_weight = weight[tap_k * channels : (tap_k + 1) * channels]
        source = g_ext[2 - tap_k : 2 - tap_k + nframes].reshape(-1, channels)
        back_sum = back_sum + lax.dot_general(
            source, tap_weight, (((1,), (1,)), ((), ())), preferred_element_type=jnp.float32
        )
    middle = y_ext[1:-1]
    back_t = (silu_grad(middle.astype(jnp.float32)) * back_sum.reshape(middle.shape)).astype(
        jnp.bfloat16
    )
    return (back_t, jnp.concatenate(grads, axis=0))


def frame_slots(counts_row, nframes, cap):
    ndevices = counts_row.shape[0]
    ends = jnp.cumsum(counts_row)
    starts = ends - counts_row
    frame_ids = jnp.arange(nframes, dtype=jnp.int32)
    owner = jnp.sum((ends[None, :] <= frame_ids[:, None]).astype(jnp.int32), axis=1)
    device_ids = jnp.arange(ndevices, dtype=jnp.int32)
    first = jnp.sum(jnp.where(device_ids[None, :] == owner[:, None], starts[None, :], 0), axis=1)
    return owner * cap + frame_ids - first


def slot_frames(counts_row, cap):
    ndevices = counts_row.shape[0]
    ends = jnp.cumsum(counts_row)
    starts = ends - counts_row
    slot_ids = jnp.arange(ndevices * cap, dtype=jnp.int32)
    device = slot_ids // cap
    inner = slot_ids % cap
    device_ids = jnp.arange(ndevices, dtype=jnp.int32)
    onehot = device[:, None] == device_ids[None, :]
    held = jnp.sum(jnp.where(onehot, counts_row[None, :], 0), axis=1)
    first = jnp.sum(jnp.where(onehot, starts[None, :], 0), axis=1)
    live = inner < held
    return (jnp.where(live, first + inner, 0), live)


def shards(frames_in, cotangent, counts, norm_gain, norm_shift, spatial_weight, temporal_weight):
    inputs = frames_in[0]
    cotan = cotangent[0]
    counts_row = counts[0]
    cap = inputs.shape[0]
    tm_size = lax.axis_size("tm")
    own_count = jnp.sum(
        jnp.where(jnp.arange(tm_size, dtype=jnp.int32) == lax.axis_index("tm"), counts_row, 0)
    )
    live_slots = (jnp.arange(cap, dtype=jnp.int32) < own_count)[:, None, None, None]

    def activate(values):
        return norm_act(values, norm_gain, norm_shift, GROUPS)

    inputs_f = inputs.astype(jnp.float32)
    act_f, act_back = jax.vjp(activate, inputs_f)
    acts = act_f.astype(jnp.bfloat16)
    mixed = spatial_conv(acts, spatial_weight)
    y_out = (inputs_f + mixed).astype(jnp.bfloat16)
    y_rows, g_rows = (
        lax.all_to_all(y_out, "tm", split_axis=1, concat_axis=0, tiled=True),
        lax.all_to_all(cotan, "tm", split_axis=1, concat_axis=0, tiled=True),
    )
    pick = frame_slots(counts_row, 2 * tm_size, cap)
    pad_spec = ((1, 1), (0, 0), (0, 0), (0, 0))
    y_ext = jnp.pad(jnp.take(y_rows, pick, axis=0), pad_spec)
    g_ext = jnp.pad(jnp.take(g_rows, pick, axis=0), pad_spec)
    back_rows, grad_part = temporal_core(y_ext, g_ext, temporal_weight)
    back_idx, live = slot_frames(counts_row, cap)
    back_slots = jnp.where(
        live[:, None, None, None],
        jnp.take(back_rows, back_idx, axis=0),
        jnp.zeros((), jnp.bfloat16),
    )
    back_t = lax.all_to_all(back_slots, "tm", split_axis=0, concat_axis=1, tiled=True)
    d_out = (cotan.astype(jnp.float32) + back_t.astype(jnp.float32)).astype(jnp.bfloat16)
    d_act = spatial_conv_t(d_out, spatial_weight)
    d_in = d_out.astype(jnp.float32) + act_back(d_act)[0]
    d_in = jnp.where(live_slots, d_in, 0.0).astype(jnp.bfloat16)
    height, width = (inputs.shape[1], inputs.shape[2])
    scale = 1.0 / math.sqrt(lax.axis_size("dp") * 2 * tm_size * height * width)
    summed = lax.psum(grad_part, ("dp", "tm"))
    return (d_in[None], summed * scale)


def solution(mesh):
    return jax.shard_map(
        shards,
        mesh=mesh,
        in_specs=(
            P("dp", "tm", None, None, None),
            P("dp", "tm", None, None, None),
            P("dp", None),
            P(),
            P(),
            P(),
            P(),
        ),
        out_specs=(P("dp", "tm", None, None, None), P()),
        check_vma=False,
    )
```

profile of v0, /device:TPU:0, one launch (start us, length us, event | category | flops | bytes accessed | tf_op | source)
XLA Modules:
  0.0 206.0 jit_solution(17394127910788598569)
XLA Ops:
  7.2 1.7 copy.41
  8.9 5.2 %all-to-all-start.1 = ((bf16[3,8,8,320]{3,2,0,1:T(8,128)(2,1)}), bf16[3,8,8,320]{3,2,0,1:T(8,128)(2,1)}, u32[]{:S(2)}, u32[]{:S(2)}) async-start(bf16[3,8,8,320]{3,2,0,1:T(8,128)(2,1)} %copy.41), calls=%async_computation.1 | async-start | bytes 294912 | tf_op jit(solution)/shard_map/all_to_all | solution.py:134
  14.0 0.8 reduce-window.4
  14.9 0.7 fusion.58
  15.5 0.7 select_reduce_fusion.2
  16.5 1.0 convert_reduce_fusion
  17.7 0.1 sub.33
  17.9 1.0 fusion.13
  19.0 0.6 divide_multiply_fusion
  19.7 0.1 rsqrt.16
  19.9 0.1 fusion.22
  20.0 0.6 copy-done.1
  20.7 1.0 pad_slice_fusion.8
  21.7 3.3 %copy.48 = bf16[2880,320]{1,0:T(8,128)(2,1)S(1)} copy(bf16[2880,320]{0,1:T(8,128)(2,1)} %param.14) | data formatting | bytes 3686400 | tf_op args[5]
  25.0 2.4 %concatenate.9 = bf16[3,8,8,2880]{3,2,1,0:T(8,128)(2,1)S(1)} concatenate(bf16[3,8,8,320]{3,2,1,0:T(8,128)(2,1)} %get-tuple-element.24, bf16[3,8,8,320]{3,2,1,0:T(8,128)(2,1)} %get-tuple-element.18, bf16[3,8,8,320]{3,2,1,0:T(8,128)(2,1)} %get-tuple-element.19, bf16[3,8,8,320]{3,2,1,0:T(8,128)(2,1)} %get-tuple-element.20, bf16[3,8,8,320]{3,2,1,0:T(8,128)(2,1)} %copy-done.1, ...), dimensions={3} | concatenate | bytes 2211840 | tf_op jit(solution)/shard_map/concatenate | solution.py:35
  27.4 2.4 %fusion.5 = bf16[3,8,8,320]{3,2,1,0:T(8,128)(2,1)S(1)} fusion(bf16[3,8,8,2880]{3,2,1,0:T(8,128)(2,1)S(1)} %concatenate.9, bf16[2880,320]{0,1:T(8,128)(2,1)} %param.14, bf16[1,3,8,8,320]{4,3,2,1,0:T(8,128)(2,1)S(1)} %copy-done), kind=kOutput, calls=%fused_computation.11 | convolution fusion | flops 354078720 | bytes 3194880 | tf_op jit(solution)/shard_map/dot_general | solution.py:41
  29.8 0.7 copy.39
  30.5 1.6 reverse_bitcast_fusion
  32.1 3.1 %copy.49 = bf16[9,320,320]{2,1,0:T(8,128)(2,1)S(1)} copy(bf16[9,320,320]{1,2,0:T(8,128)(2,1)} %reverse_bitcast_fusion) | data formatting | bytes 3686400 | tf_op jit(solution)/shard_map/transpose | solution.py:50
  35.2 0.6 fusion.57
  35.8 1.1 iota_compare_fusion.3
  37.0 4.2 %all-to-all-start = ((bf16[3,8,8,320]{3,2,0,1:T(8,128)(2,1)}), bf16[3,8,8,320]{3,2,0,1:T(8,128)(2,1)}, u32[]{:S(2)}, u32[]{:S(2)}) async-start(bf16[3,8,8,320]{3,2,0,1:T(8,128)(2,1)} %copy.39), calls=%async_computation | async-start | bytes 294912 | tf_op jit(solution)/shard_map/all_to_all | solution.py:133
  41.2 1.5 gather_fusion.2
  42.7 0.3 fusion.34
  43.0 0.4 convolution_add_fusion.1
  43.4 0.3 convolution_add_fusion
  43.8 0.1 copy.42
  44.0 3.0 %all-to-all-done = bf16[3,8,8,320]{3,2,0,1:T(8,128)(2,1)} async-done(((bf16[3,8,8,320]{3,2,0,1:T(8,128)(2,1)}), bf16[3,8,8,320]{3,2,0,1:T(8,128)(2,1)}, u32[]{:S(2)}, u32[]{:S(2)}) %all-to-all-start) | async-done | bytes 122912 | tf_op jit(solution)/shard_map/all_to_all | solution.py:133
  47.0 1.5 gather_fusion.1
  48.5 0.2 fusion.52
  48.7 0.3 convolution_bitcast_fusion
  49.0 0.3 convolution_bitcast_fusion.1
  49.3 1.1 convolution_bitcast_fusion.2
  50.4 1.2 gather_fusion
  51.6 1.7 fusion.45
  53.3 3.4 %all-to-all-start.2 = ((bf16[24,1,8,320]{3,2,1,0:T(8,128)(2,1)}), bf16[24,1,8,320]{3,2,1,0:T(8,128)(2,1)S(1)}, u32[]{:S(2)}, u32[]{:S(2)}) async-start(bf16[24,1,8,320]{3,2,1,0:T(8,128)(2,1)} %fusion.45), calls=%async_computation.2 | async-start | bytes 294912 | tf_op jit(solution)/shard_map/all_to_all | solution.py:147
  56.7 2.3 %pad_maximum_fusion = f32[960,320]{0,1:T(8,128)} fusion(f32[320,320]{0,1:T(8,128)S(1)} %convolution_bitcast_fusion, f32[320,320]{0,1:T(8,128)S(1)} %convolution_bitcast_fusion.1, f32[320,320]{0,1:T(8,128)} %convolution_bitcast_fusion.2), kind=kLoop, calls=%fused_computation.6 | loop fusion | flops 614400 | bytes 2457600 | tf_op jit(solution)/shard_map/concatenate | solution.py:84
  59.1 3.2 %all-to-all-done.2 = bf16[24,1,8,320]{3,2,1,0:T(8,128)(2,1)S(1)} async-done(((bf16[24,1,8,320]{3,2,1,0:T(8,128)(2,1)}), bf16[24,1,8,320]{3,2,1,0:T(8,128)(2,1)S(1)}, u32[]{:S(2)}, u32[]{:S(2)}) %all-to-all-start.2) | async-done | bytes 122912 | tf_op jit(solution)/shard_map/all_to_all | solution.py:147
  62.4 0.8 pad_slice_fusion
  63.2 2.7 %concatenate.10 = bf16[3,8,8,2880]{3,2,1,0:T(8,128)(2,1)} concatenate(bf16[3,8,8,320]{3,2,1,0:T(8,128)(2,1)} %get-tuple-element.16, bf16[3,8,8,320]{3,2,1,0:T(8,128)(2,1)S(1)} %get-tuple-element.10, bf16[3,8,8,320]{3,2,1,0:T(8,128)(2,1)S(1)} %get-tuple-element.11, bf16[3,8,8,320]{3,2,1,0:T(8,128)(2,1)S(1)} %get-tuple-element.12, bf16[3,8,8,320]{3,2,1,0:T(8,128)(2,1)S(1)} %fusion.31, ...), dimensions={3} | concatenate | bytes 2211840 | tf_op jit(solution)/shard_map/concatenate | solution.py:35
  65.9 2.1 %fusion.26 = (f32[3,320]{1,0:T(4,128)S(1)}, f32[3,8,8,320]{3,2,1,0:T(8,128)S(1)}) fusion(bf16[1,3,8,8,320]{4,3,2,1,0:T(8,128)(2,1)S(1)} %copy-done, f32[3,320]{1,0:T(4,128)S(1)} %sub.33, f32[320]{0:T(512)} %param.13, f32[320]{0:T(512)} %param.12, f32[3,320]{1,0:T(4,128)S(1)} %rsqrt.16, bf16[3,8,8,2880]{3,2,1,0:T(8,128)(2,1)} %concatenate.10, ...), kind=kOutput, calls=%fused_computation.55 | convolution fusion | flops 354937920 | bytes 3331840 | tf_op jit(solution)/shard_map/dot_general | solution.py:41
  68.0 0.1 reduce_sum.137
  68.1 0.2 multiply_reduce_fusion
  68.4 0.1 reshape.221
  68.9 0.1 reshape.222
  69.0 0.8 fusion.43
  69.8 126.9 %all-reduce.6.cloned.1.call-done = f32[960,320]{0,1:T(8,128)} async-done(((f32[960,320]{0,1:T(8,128)}), f32[960,320]{0,1:T(8,128)}) %all-reduce.6.cloned.1.call-update) | async-done | bytes 1228816 | tf_op jit(solution)/shard_map/psum | solution.py:154
  196.7 2.5 %broadcast_multiply_fusion = f32[960,320]{0,1:T(8,128)} fusion(f32[960,320]{0,1:T(8,128)} %all-reduce.6.cloned.1.call-done), kind=kLoop, calls=%fused_computation.30 | loop fusion | flops 307200 | bytes 2457600 | tf_op jit(solution)/shard_map/mul | solution.py:155
  (47 shorter events, 1.7 us)
Async XLA Ops:
  7.2 12.7 %copy-start = (bf16[1,3,8,8,320]{4,3,2,1,0:T(8,128)(2,1)S(1)}, bf16[1,3,8,8,320]{4,3,2,1,0:T(8,128)(2,1)}, u32[]{:S(2)}) copy-start(bf16[1,3,8,8,320]{4,3,2,1,0:T(8,128)(2,1)} %param.9) | copy-start | bytes 368644
  7.2 12.7 %copy-start.5 = (f32[320]{0:T(512)S(1)}, f32[320]{0:T(512)}, u32[]{:S(2)}) copy-start(f32[320]{0:T(512)} %param.13) | copy-start | bytes 3844
  7.2 12.7 %copy-start.6 = (f32[320]{0:T(512)S(1)}, f32[320]{0:T(512)}, u32[]{:S(2)}) copy-start(f32[320]{0:T(512)} %param.12) | copy-start | bytes 3844
  8.9 28.1 %all-to-all-start.1 = ((bf16[3,8,8,320]{3,2,0,1:T(8,128)(2,1)}), bf16[3,8,8,320]{3,2,0,1:T(8,128)(2,1)}, u32[]{:S(2)}, u32[]{:S(2)}) async-start(bf16[3,8,8,320]{3,2,0,1:T(8,128)(2,1)} %copy.41), calls=%async_computation.1 | async-start | bytes 294912 | tf_op jit(solution)/shard_map/all_to_all | solution.py:134
  20.0 0.6 copy-start.1
  32.1 3.1 %copy-start.7 = (s32[1,8]{1,0:T(1,128)S(1)}, s32[1,8]{1,0:T(1,128)}, u32[]{:S(2)}) copy-start(s32[1,8]{1,0:T(1,128)} %param.11) | copy-start | bytes 100
  32.1 10.6 %copy-start.2 = (bf16[960,320]{0,1:T(8,128)(2,1)S(1)}, bf16[960,320]{0,1:T(8,128)(2,1)}, u32[]{:S(2)}) copy-start(bf16[960,320]{0,1:T(8,128)(2,1)} %param.15) | copy-start | bytes 1843204
  37.0 10.0 %all-to-all-start = ((bf16[3,8,8,320]{3,2,0,1:T(8,128)(2,1)}), bf16[3,8,8,320]{3,2,0,1:T(8,128)(2,1)}, u32[]{:S(2)}, u32[]{:S(2)}) async-start(bf16[3,8,8,320]{3,2,0,1:T(8,128)(2,1)} %copy.39), calls=%async_computation | async-start | bytes 294912 | tf_op jit(solution)/shard_map/all_to_all | solution.py:133
  53.3 9.0 %all-to-all-start.2 = ((bf16[24,1,8,320]{3,2,1,0:T(8,128)(2,1)}), bf16[24,1,8,320]{3,2,1,0:T(8,128)(2,1)S(1)}, u32[]{:S(2)}, u32[]{:S(2)}) async-start(bf16[24,1,8,320]{3,2,1,0:T(8,128)(2,1)} %fusion.45), calls=%async_computation.2 | async-start | bytes 294912 | tf_op jit(solution)/shard_map/all_to_all | solution.py:147
  56.7 140.0 %all-reduce.6.cloned.1.call-start = ((), (), s32[]{:S(2)}) async-start(), calls=%async_computation.3 | async-start | bytes 2621440 | tf_op jit(solution)/shard_map/psum | solution.py:154
  59.1 3.2 %copy-start.3 = (bf16[1,3,8,8,320]{4,3,2,1,0:T(8,128)(2,1)S(1)}, bf16[1,3,8,8,320]{4,3,2,1,0:T(8,128)(2,1)}, u32[]{:S(2)}) copy-start(bf16[1,3,8,8,320]{4,3,2,1,0:T(8,128)(2,1)} %param.10) | copy-start | bytes 368644
  65.9 2.2 %copy-start.4 = (f32[3,32]{1,0:T(4,128)S(1)}, f32[3,32]{1,0:T(4,128)}, u32[]{:S(2)}) copy-start(f32[3,32]{1,0:T(4,128)} %get-tuple-element.25) | copy-start | bytes 1156
  65.9 3.1 %copy-start.8 = (pred[3]{0:T(512)(128)(4,1)S(1)}, pred[3]{0:T(512)(128)(4,1)}, u32[]{:S(2)}) copy-start(pred[3]{0:T(512)(128)(4,1)} %iota_compare_fusion.3) | copy-start | bytes 13
Sparse Core Ops, SparseCore 0:
  63.5 133.1 all-reduce.5
where the time goes:
time: 207 us; the launch traced here: 206 us
  waiting for transfers between devices  133 us (64%)
  local copies, waits for them, and re-layouts  23.5 us (11%)
  other arithmetic  15.2 us (7%)
  between operations  14.3 us (7%)
  starting transfers between devices  12.8 us (6%)
  matrix products  7.04 us (3%)
    psum x1, waiting for transfers between devices, shards(): summed = lax.psum(grad_part, ('dp', 'tm'))  127 us
    all_to_all x1, starting transfers between devices, shards(): lax.all_to_all(cotan, 'tm', split_axis=1, concat_axis=0, tiled=True)  5.17 us
    concatenate x2, local copies, waits for them, and re-layouts, patches(): return jnp.concatenate(pieces, axis=3)  5.12 us
    transpose x2, local copies, waits for them, and re-layouts, spatial_conv_t(): weight.reshape(9, -1, channels)[::-1].transpose(0, 2, 1)  4.69 us
    dot_general x2, matrix products, spatial_conv(): jnp.dot(stacked.reshape(-1, stacked.shape[3]), weight, preferred_element_...  4.47 us
    all_to_all x1, starting transfers between devices, shards(): lax.all_to_all(y_out, 'tm', split_axis=1, concat_axis=0, tiled=True)  4.2 us
  transfers between devices with their start and end apart: 4, of which 3 were waited for; matrix products, arithmetic and copies ran while one was open for 17% of the time, Pallas kernels for 0%

commit v1 on v0

--- a/solution.py
+++ b/solution.py
@@ -3,6 +3,8 @@
 import jax
 import jax.numpy as jnp
 from jax import lax
+from jax.experimental import pallas as pl
+from jax.experimental.pallas import tpu as pltpu
 from jax.sharding import PartitionSpec as P
 
 GROUPS = 32
@@ -155,9 +157,328 @@
     return (d_in[None], summed * scale)
 
 
+CAP = 3
+SIDE = 8
+CH = 320
+PIX = SIDE * SIDE
+ROWS = CAP * PIX
+LANE = 128
+UNITS = 8
+BLOCK = 80
+CHUNKS = 32
+F32 = jnp.float32
+BF16 = jnp.bfloat16
+
+
+def dot(a, b, ca, cb):
+    return lax.dot_general(a, b, (((ca,), (cb,)), ((), ())), preferred_element_type=F32)
+
+
+def group_matrix():
+    def ids(axis):
+        index = lax.broadcasted_iota(jnp.int32, (CH, CH), axis).astype(F32)
+        return jnp.floor((index + 0.5) * (GROUPS / CH))
+
+    return (ids(0) == ids(1)).astype(BF16)
+
+
+def group_means(totals, members):
+    rows = jnp.concatenate(totals, axis=0)
+    high = rows.astype(BF16)
+    rest = rows - high.astype(F32)
+    mid = rest.astype(BF16)
+    low = (rest - mid.astype(F32)).astype(BF16)
+    summed = dot(high, members, 1, 0) + dot(mid, members, 1, 0) + dot(low, members, 1, 0)
+    return summed * (1.0 / (PIX * (CH // GROUPS)))
+
+
+def frame_of(value, frame):
+    return value[frame * PIX : (frame + 1) * PIX]
+
+
+def column_sum(value):
+    return jnp.sum(value, axis=0, keepdims=True)
+
+
+def sigmoid(value):
+    return 1.0 / (1.0 + jnp.exp(-value))
+
+
+def stage_shifts(value, line, padded):
+    column = lax.broadcasted_iota(jnp.int32, (ROWS, CH), 0) % SIDE
+    line[8 : 8 + ROWS, :] = value
+    left = jnp.where(column == 0, 0.0, line[7 : 7 + ROWS, :])
+    right = jnp.where(column == SIDE - 1, 0.0, line[9 : 9 + ROWS, :])
+    for j, moved in enumerate((left, value, right)):
+        padded[j, :, 1 : 1 + SIDE] = moved.reshape(CAP, SIDE, SIDE, CH)
+
+
+def shifted(padded, j, i):
+    return padded[j, :, i : i + SIDE].reshape(ROWS, CH).astype(BF16)
+
+
+def fused_kernel(
+    counts, x_ref, g_ref, gain_ref, shift_ref, ws_hbm, wt_hbm, out_ref, grad_ref,
+    ws, wt, line, padded, edge, halo, part, part16, from_core, quad16, from_plane, own16, from_z, full,
+    weight_sem, halo_send, halo_recv, core_sem, plane_send, plane_recv, z_send, z_recv,
+    gather_send, gather_z, gather_plane, gather_core,
+):
+    dp = lax.axis_index("dp")
+    tm = lax.axis_index("tm")
+    yy, xx, core = tm // 4, (tm // 2) % 2, tm % 2
+    chip = tm // 2
+
+    def at(z, chip_id, core_id):
+        return (z, chip_id * 2 + core_id)
+
+    plane = [yy * 2 + (1 - xx), (1 - yy) * 2 + xx, (1 - yy) * 2 + (1 - xx)]
+    z_to = [lax.rem(dp + d, 4) for d in (1, 2, 3)]
+    z_from = [lax.rem(dp + 4 - d, 4) for d in (1, 2, 3)]
+    before, after = lax.rem(tm + 7, 8), lax.rem(tm + 1, 8)
+    partner = at(dp, chip, 1 - core)
+    peers = [(dp, before), (dp, after)] + [at(dp, p, core) for p in plane] + [at(z, chip, core) for z in z_to]
+
+    def remote(src, dst, send_sem, recv_sem, device):
+        copy = pltpu.make_async_remote_copy(
+            src_ref=src, dst_ref=dst, send_sem=send_sem, recv_sem=recv_sem,
+            device_id=device, device_id_type=pl.DeviceIdType.MESH,
+        )
+        return copy
+
+    barrier = pltpu.get_barrier_semaphore()
+    for peer in peers:
+        pl.semaphore_signal(barrier, inc=1, device_id=peer, device_id_type=pl.DeviceIdType.MESH)
+    load_s = pltpu.make_async_copy(ws_hbm, ws, weight_sem.at[0])
+    load_t = pltpu.make_async_copy(wt_hbm, wt, weight_sem.at[1])
+    load_s.start()
+    load_t.start()
+
+    count = counts[0, tm]
+    g16 = g_ref[...]
+    g = g16.astype(F32)
+    g_frames = [frame_of(g, s) for s in range(CAP)]
+    last = jnp.where(count == 3, g_frames[2], jnp.where(count == 2, g_frames[1], g_frames[0]))
+    edge[0] = g_frames[0].astype(BF16)
+    edge[1] = last.astype(BF16)
+    pl.semaphore_wait(barrier, len(peers))
+    halo_copies = [
+        remote(edge.at[0], halo.at[1], halo_send.at[0], halo_recv.at[1], (dp, before)),
+        remote(edge.at[1], halo.at[0], halo_send.at[1], halo_recv.at[0], (dp, after)),
+    ]
+    for copy in halo_copies:
+        copy.start()
+
+    members = group_matrix()
+    gain, shift = gain_ref[...], shift_ref[...]
+    x = x_ref[...].astype(F32)
+    x_frames = [frame_of(x, s) for s in range(CAP)]
+    means = group_means([column_sum(v) for v in x_frames], members)
+    centred = [v - means[s : s + 1] for s, v in enumerate(x_frames)]
+    spread = group_means([column_sum(v * v) for v in centred], members)
+    inverse = lax.rsqrt(spread + 1e-05)
+    xhat = jnp.concatenate([v * inverse[s : s + 1] for s, v in enumerate(centred)], axis=0)
+    normed = xhat * gain + shift
+    sig_n = sigmoid(normed)
+    padded[...] = jnp.zeros_like(padded)
+    stage_shifts(normed * sig_n, line, padded)
+
+    load_s.wait()
+    mixed = jnp.zeros((ROWS, CH), F32)
+    for tap in range(9):
+        mixed = mixed + dot(shifted(padded, tap % 3, tap // 3), ws[:, tap * CH : (tap + 1) * CH], 1, 1)
+    y = (x + mixed).astype(BF16).astype(F32)
+    sig_y = sigmoid(y)
+    slot = lax.broadcasted_iota(jnp.int32, (ROWS, CH), 0) // PIX
+    live = slot < count
+    u = jnp.where(live, y * sig_y, 0.0).astype(BF16)
+
+    for copy in halo_copies:
+        copy.wait()
+    prev_edge = jnp.where(tm == 0, 0.0, halo[0].astype(F32))
+    next_edge = jnp.where(tm == 7, 0.0, halo[1].astype(F32))
+    g_prev = jnp.concatenate([prev_edge, g_frames[0], g_frames[1]], axis=0).astype(BF16)
+    g_next = jnp.concatenate(
+        [
+            jnp.where(count == 1, next_edge, g_frames[1]),
+            jnp.where(count == 2, next_edge, g_frames[2]),
+            next_edge,
+        ],
+        axis=0,
+    ).astype(BF16)
+    taps = (g_next, g16, g_prev)
+
+    none = jnp.zeros((ROWS, 64), BF16)
+    u_low = jnp.concatenate([u, none], axis=1)
+    u_high = jnp.concatenate([none, u], axis=1)
+    t0 = dot(taps[0], u_low, 0, 0)
+    t1 = dot(taps[1], u_high, 0, 0)
+    t2 = dot(taps[2], u_low, 0, 0)
+    units = [
+        t0[:, 0:128], t0[:, 128:256], t0[:, 256:384] + t1[:, 0:128], t1[:, 128:256], t1[:, 256:384],
+        t2[:, 0:128], t2[:, 128:256], t2[:, 256:384],
+    ]
+    for r in range(4):
+        for l in range(UNITS):
+            piece = units[l][r * BLOCK : (r + 1) * BLOCK]
+            part[r * UNITS + l] = piece
+            part16[r * UNITS + l] = piece.astype(BF16)
+
+    core_copy = remote(part16.at[pl.ds((1 - core) * 16, 16)], from_core, core_sem.at[0], core_sem.at[1], partner)
+    core_copy.start()
+
+    load_t.wait()
+    du = jnp.zeros((ROWS, CH), F32)
+    for k in range(3):
+        du = du + dot(taps[k], wt[:, k * CH : (k + 1) * CH], 1, 0)
+    back_t = (sig_y * (1.0 + y * (1.0 - sig_y)) * du).astype(BF16).astype(F32)
+    dy = jnp.where(live, (g + back_t).astype(BF16).astype(F32), 0.0)
+
+    core_copy.wait()
+    quad = part[pl.ds(core * 16, 16)] + from_core[...].astype(F32)
+    part[pl.ds(core * 16, 16)] = quad
+    quad16[...] = quad.astype(BF16)
+    plane_copies = [
+        remote(quad16.at[pl.ds(p * 4, 4)], from_plane.at[d], plane_send.at[d], plane_recv.at[d], at(dp, p, core))
+        for d, p in enumerate(plane)
+    ]
+    for copy in plane_copies:
+        copy.start()
+
+    stage_shifts(dy, line, padded)
+    da = jnp.zeros((ROWS, CH), F32)
+    for tap in range(9):
+        da = da + dot(shifted(padded, 2 - tap % 3, 2 - tap // 3), ws[:, tap * CH : (tap + 1) * CH], 1, 0)
+
+    for copy in plane_copies:
+        copy.wait()
+    first = core * 16 + chip * 4
+    four = part[pl.ds(first, 4)] + from_plane[0].astype(F32) + from_plane[1].astype(F32) + from_plane[2].astype(F32)
+    part[pl.ds(first, 4)] = four
+    own16[...] = four.astype(BF16)
+    z_copies = [
+        remote(own16.at[z], from_z.at[d], z_send.at[d], z_recv.at[d], at(z, chip, core))
+        for d, z in enumerate(z_to)
+    ]
+    for copy in z_copies:
+        copy.start()
+
+    dhat = da * (sig_n * (1.0 + normed * (1.0 - sig_n))) * gain
+    dhat_frames = [frame_of(dhat, s) for s in range(CAP)]
+    xhat_frames = [frame_of(xhat, s) for s in range(CAP)]
+    mean_d = group_means([column_sum(v) for v in dhat_frames], members)
+    mean_dx = group_means([column_sum(v * w) for v, w in zip(dhat_frames, xhat_frames)], members)
+    dx = jnp.concatenate(
+        [
+            inverse[s : s + 1] * (dhat_frames[s] - mean_d[s : s + 1] - xhat_frames[s] * mean_dx[s : s + 1])
+            for s in range(CAP)
+        ],
+        axis=0,
+    )
+    out_ref[...] = jnp.where(live, dy + dx, 0.0).astype(BF16)
+
+    for copy in z_copies:
+        copy.wait()
+    mine = first + dp
+    total = part[mine] + from_z[0].astype(F32) + from_z[1].astype(F32) + from_z[2].astype(F32)
+    full[mine] = total.astype(BF16)
+
+    sent = []
+
+    def pass_on(chunk, sem_id, device, recv_sem):
+        copy = remote(full.at[chunk], full.at[chunk], gather_send.at[sem_id], recv_sem, device)
+        copy.start()
+        sent.append(copy)
+
+    for d, z in enumerate(z_to):
+        pass_on(mine, d, at(z, chip, core), gather_z.at[d])
+    for d, p in enumerate(plane):
+        pass_on(mine, 3 + d, at(dp, p, core), gather_plane.at[d])
+    pass_on(mine, 6, partner, gather_core.at[0])
+    for k, z in enumerate(z_from):
+        chunk = first + z
+        remote(full.at[chunk], full.at[chunk], gather_send.at[0], gather_z.at[k], partner).wait_recv()
+        for d, p in enumerate(plane):
+            pass_on(chunk, 7 + k * 4 + d, at(dp, p, core), gather_plane.at[(k + 1) * 3 + d])
+        pass_on(chunk, 7 + k * 4 + 3, partner, gather_core.at[k + 1])
+    sem_id = 19
+    for k, z in enumerate([dp] + z_from):
+        for d, p in enumerate(plane):
+            chunk = core * 16 + p * 4 + z
+            remote(full.at[chunk], full.at[chunk], gather_send.at[0], gather_plane.at[k * 3 + d], partner).wait_recv()
+            pass_on(chunk, sem_id, partner, gather_core.at[4 + k * 3 + d])
+            sem_id = sem_id + 1
+    others = [chip] + plane
+    for k, z in enumerate([dp] + z_from):
+        for d, p in enumerate(others):
+            chunk = (1 - core) * 16 + p * 4 + z
+            slot_id = k if d == 0 else 4 + k * 3 + d - 1
+            remote(full.at[chunk], full.at[chunk], gather_send.at[0], gather_core.at[slot_id], partner).wait_recv()
+    for copy in sent:
+        copy.wait_send()
+
+    scale = 1.0 / math.sqrt(4 * 2 * 8 * PIX)
+    for r in range(4):
+        for l in range(UNITS):
+            width = min(LANE, 3 * CH - l * LANE)
+            value = full[r * UNITS + l].astype(F32) * scale
+            grad_ref[r * BLOCK : (r + 1) * BLOCK, l * LANE : l * LANE + width] = value[:, :width]
+
+
+def fused_shards(frames_in, cotangent, counts, norm_gain, norm_shift, spatial_weight, temporal_weight):
+    vmem = pl.BlockSpec(memory_space=pltpu.VMEM)
+    hbm = pl.BlockSpec(memory_space=pl.ANY)
+    dma = pltpu.SemaphoreType.DMA
+    out, grad = pl.pallas_call(
+        fused_kernel,
+        out_shape=(
+            jax.ShapeDtypeStruct((ROWS, CH), BF16),
+            jax.ShapeDtypeStruct((CH, 3 * CH), F32),
+        ),
+        in_specs=[pl.BlockSpec(memory_space=pltpu.SMEM), vmem, vmem, vmem, vmem, hbm, hbm],
+        out_specs=(vmem, vmem),
+        scratch_shapes=[
+            pltpu.VMEM((CH, 9 * CH), BF16),
+            pltpu.VMEM((CH, 3 * CH), BF16),
+            pltpu.VMEM((ROWS + 16, CH), F32),
+            pltpu.VMEM((3, CAP, SIDE + 2, SIDE, CH), F32),
+            pltpu.VMEM((2, PIX, CH), BF16),
+            pltpu.VMEM((2, PIX, CH), BF16),
+            pltpu.VMEM((CHUNKS, BLOCK, LANE), F32),
+            pltpu.VMEM((CHUNKS, BLOCK, LANE), BF16),
+            pltpu.VMEM((16, BLOCK, LANE), BF16),
+            pltpu.VMEM((16, BLOCK, LANE), BF16),
+            pltpu.VMEM((3, 4, BLOCK, LANE), BF16),
+            pltpu.VMEM((4, BLOCK, LANE), BF16),
+            pltpu.VMEM((3, BLOCK, LANE), BF16),
+            pltpu.VMEM((CHUNKS, BLOCK, LANE), BF16),
+            dma((2,)), dma((2,)), dma((2,)), dma((2,)), dma((3,)), dma((3,)), dma((3,)), dma((3,)),
+            dma((31,)), dma((3,)), dma((12,)), dma((16,)),
+        ],
+        compiler_params=pltpu.CompilerParams(
+            collective_id=0, has_side_effects=True, vmem_limit_bytes=40 * 1024 * 1024
+        ),
+    )(
+        counts,
+        frames_in.reshape(ROWS, CH),
+        cotangent.reshape(ROWS, CH),
+        norm_gain.reshape(1, CH),
+        norm_shift.reshape(1, CH),
+        spatial_weight.T,
+        temporal_weight.T,
+    )
+    return out.reshape(frames_in.shape), grad.T
+
+
 def solution(mesh):
+    fused = mesh.shape["dp"] == 4 and mesh.shape["tm"] == 8
+
+    def block(frames_in, *rest):
+        if fused and frames_in.shape == (1, CAP, SIDE, SIDE, CH):
+            return fused_shards(frames_in, *rest)
+        return shards(frames_in, *rest)
+
     return jax.shard_map(
-        shards,
+        block,
         mesh=mesh,
         in_specs=(
             P("dp", "tm", None, None, None),

time: 207 us -> 40.6 us (0.20)
  waiting for transfers between devices: 133 us -> 0 us
  Pallas kernels: 0 us -> 31.5 us
  local copies, waits for them, and re-layouts: 23.5 us -> 8.16 us
  other arithmetic: 15.2 us -> 0 us
  between operations: 14.3 us -> 0.64 us
  starting transfers between devices: 12.8 us -> 0 us
  matrix products: 7.04 us -> 0 us
    psum x1 -> x0, waiting for transfers between devices: 127 us -> none  [shards(): summed = lax.psum(grad_part, ('dp', 'tm'))]
    pallas_call x0 -> x1, Pallas kernels: none -> 31.5 us  [fused_shards(): pl.pallas_call(fused_kernel, out_shape=(jax.ShapeDtypeStruct((ROWS, CH),...]
    all_to_all x3 -> x0, starting transfers between devices: 12.7 us -> none  [the longest x1 5.17 us: shards(): lax.all_to_all(cotan, 'tm', split_axis=1, concat_axis=0, tiled=True)]
    dot_general x8 -> x0, matrix products: 7.04 us -> none  [the longest x2 4.47 us: spatial_conv(): jnp.dot(stacked.reshape(-1, stacked.shape[3]), weight, preferred_element_...]
    all_to_all x3 -> x0, waiting for transfers between devices: 6.23 us -> none  [the longest x1 3.22 us: shards(): lax.all_to_all(back_slots, 'tm', split_axis=0, concat_axis=1, tiled=True)]
    concatenate x2 -> x0, local copies, waits for them, and re-layouts: 5.12 us -> none  [patches(): return jnp.concatenate(pieces, axis=3)]
    transpose x2 -> x0, local copies, waits for them, and re-layouts: 4.69 us -> none  [spatial_conv_t(): weight.reshape(9, -1, channels)[::-1].transpose(0, 2, 1)]
    gather x3 -> x0, local copies, waits for them, and re-layouts: 4.21 us -> none  [the longest x1 1.49 us: shards(): y_ext = jnp.pad(jnp.take(y_rows, pick, axis=0), pad_spec)]
  transfers between devices with their start and end apart: 4 -> 0, of which waited for: 3 -> 0; matrix products, arithmetic and copies ran while one was open for 17% -> 0% of each run, Pallas kernels for 0% -> 0%
where the time goes in v1:
time: 40.6 us; the launch traced here: 40.3 us
  Pallas kernels  31.5 us (78%)
  local copies, waits for them, and re-layouts  8.16 us (20%)
  between operations  0.64 us (2%)
    pallas_call x1, Pallas kernels, fused_shards(): pl.pallas_call(fused_kernel, out_shape=(jax.ShapeDtypeStruct((ROWS, CH),...  31.5 us
    unnamed x12, local copies, waits for them, and re-layouts  6.8 us

profile of v1, /device:TPU:0, one launch (start us, length us, event | category | flops | bytes accessed | tf_op | source)
XLA Modules:
  0.0 40.3 jit_solution(2807714761013078663)
XLA Ops:
  0.6 0.7 %reshape.21.gain_ref = f32[1,320]{1,0:T(1,128)S(1)} reshape(f32[320]{0:T(512)} %param.10) | data formatting | bytes 2560 | tf_op jit(solution)/shard_map/reshape | solution.py:464
  1.3 0.7 %reshape.22.shift_ref = f32[1,320]{1,0:T(1,128)S(1)} reshape(f32[320]{0:T(512)} %param.11) | data formatting | bytes 2560 | tf_op jit(solution)/shard_map/reshape | solution.py:465
  2.0 0.0 copy-start
  2.0 1.5 %copy-done = bf16[2880,320]{0,1:T(8,128)(2,1)S(1)} copy-done((bf16[2880,320]{0,1:T(8,128)(2,1)S(1)}, bf16[2880,320]{0,1:T(8,128)(2,1)}, u32[]{:S(2)}) %copy-start) | copy-done | bytes 1843224
  3.5 0.0 copy-start.1
  3.5 1.1 %copy-done.1 = bf16[960,320]{0,1:T(8,128)(2,1)S(1)} copy-done((bf16[960,320]{0,1:T(8,128)(2,1)S(1)}, bf16[960,320]{0,1:T(8,128)(2,1)}, u32[]{:S(2)}) %copy-start.1) | copy-done | bytes 614424
  4.6 0.0 copy-start.2
  4.6 0.9 %copy-done.2 = bf16[1,3,8,8,320]{4,3,2,1,0:T(8,128)(2,1)S(1)} copy-done((bf16[1,3,8,8,320]{4,3,2,1,0:T(8,128)(2,1)S(1)}, bf16[1,3,8,8,320]{4,3,2,1,0:T(8,128)(2,1)}, u32[]{:S(2)}) %copy-start.2) | copy-done | bytes 122904
  5.5 0.0 copy-start.3
  5.5 0.9 %copy-done.3 = bf16[1,3,8,8,320]{4,3,2,1,0:T(8,128)(2,1)S(1)} copy-done((bf16[1,3,8,8,320]{4,3,2,1,0:T(8,128)(2,1)S(1)}, bf16[1,3,8,8,320]{4,3,2,1,0:T(8,128)(2,1)}, u32[]{:S(2)}) %copy-start.3) | copy-done | bytes 122904
  6.4 0.0 copy-start.4
  6.4 0.7 %copy-done.4 = s32[1,8]{1,0:T(1,128)S(1)} copy-done((s32[1,8]{1,0:T(1,128)S(1)}, s32[1,8]{1,0:T(1,128)}, u32[]{:S(2)}) %copy-start.4) | copy-done | bytes 56
  7.1 31.5 %shard_map.86 = (bf16[192,320]{1,0:T(8,128)(2,1)S(1)}, f32[320,960]{1,0:T(8,128)S(1)}) custom-call(s32[1,8]{1,0:T(1,128)S(1)} %copy-done.4, bf16[192,320]{1,0:T(8,128)(2,1)S(1)} %bitcast.9, bf16[192,320]{1,0:T(8,128)(2,1)S(1)} %bitcast.10, f32[1,320]{1,0:T(1,128)S(1)} %reshape.21.gain_ref, f32[1,320]{1,0:T(1,128)S(1)} %reshape.22.shift_ref, ...), custom_call_target="tpu_custom_call" | custom-call | tf_op jit(solution)/shard_map/pallas_call | solution.py:431
  38.6 0.7 %copy.11 = bf16[1,3,8,8,320]{4,3,2,1,0:T(8,128)(2,1)} copy(bf16[1,3,8,8,320]{4,3,2,1,0:T(8,128)(2,1)S(1)} %bitcast.11) | data formatting | bytes 245760
  39.2 1.1 %copy.12 = f32[960,320]{0,1:T(8,128)} copy(f32[960,320]{0,1:T(8,128)S(1)} %bitcast.7) | data formatting | bytes 2457600
Async XLA Ops:
  2.0 1.5 %copy-start = (bf16[2880,320]{0,1:T(8,128)(2,1)S(1)}, bf16[2880,320]{0,1:T(8,128)(2,1)}, u32[]{:S(2)}) copy-start(bf16[2880,320]{0,1:T(8,128)(2,1)} %param.12) | copy-start | bytes 5529604
  3.5 1.1 %copy-start.1 = (bf16[960,320]{0,1:T(8,128)(2,1)S(1)}, bf16[960,320]{0,1:T(8,128)(2,1)}, u32[]{:S(2)}) copy-start(bf16[960,320]{0,1:T(8,128)(2,1)} %param.13) | copy-start | bytes 1843204
  4.6 0.9 %copy-start.2 = (bf16[1,3,8,8,320]{4,3,2,1,0:T(8,128)(2,1)S(1)}, bf16[1,3,8,8,320]{4,3,2,1,0:T(8,128)(2,1)}, u32[]{:S(2)}) copy-start(bf16[1,3,8,8,320]{4,3,2,1,0:T(8,128)(2,1)} %param.7) | copy-start | bytes 368644
  5.5 0.9 %copy-start.3 = (bf16[1,3,8,8,320]{4,3,2,1,0:T(8,128)(2,1)S(1)}, bf16[1,3,8,8,320]{4,3,2,1,0:T(8,128)(2,1)}, u32[]{:S(2)}) copy-start(bf16[1,3,8,8,320]{4,3,2,1,0:T(8,128)(2,1)} %param.8) | copy-start | bytes 368644
  6.4 0.7 %copy-start.4 = (s32[1,8]{1,0:T(1,128)S(1)}, s32[1,8]{1,0:T(1,128)}, u32[]{:S(2)}) copy-start(s32[1,8]{1,0:T(1,128)} %counts.1) | copy-start | bytes 100

commit v2 on v1

--- a/solution.py
+++ b/solution.py
@@ -218,9 +218,9 @@
 
 
 def fused_kernel(
-    counts, x_ref, g_ref, gain_ref, shift_ref, ws_hbm, wt_hbm, out_ref, grad_ref,
-    ws, wt, line, padded, edge, halo, part, part16, from_core, quad16, from_plane, own16, from_z, full,
-    weight_sem, halo_send, halo_recv, core_sem, plane_send, plane_recv, z_send, z_recv,
+    counts_hbm, x_hbm, g_hbm, gain_hbm, shift_hbm, ws_hbm, wt_hbm, out_ref, grad_ref,
+    counts, x_ref, g_ref, gain_ref, shift_ref, ws, wt, line, padded, edge, halo, part, part16, from_core, quad16, from_plane, own, own16, from_z, full,
+    weight_sem, halo_send, halo_recv, core_send, core_recv, plane_send, plane_recv, z_send, z_recv,
     gather_send, gather_z, gather_plane, gather_core,
 ):
     dp = lax.axis_index("dp")
@@ -248,28 +248,31 @@
     barrier = pltpu.get_barrier_semaphore()
     for peer in peers:
         pl.semaphore_signal(barrier, inc=1, device_id=peer, device_id_type=pl.DeviceIdType.MESH)
-    load_s = pltpu.make_async_copy(ws_hbm, ws, weight_sem.at[0])
-    load_t = pltpu.make_async_copy(wt_hbm, wt, weight_sem.at[1])
-    load_s.start()
-    load_t.start()
+    places = [
+        (g_hbm, g_ref), (counts_hbm, counts), (x_hbm, x_ref), (gain_hbm, gain_ref), (shift_hbm, shift_ref),
+        (ws_hbm, ws), (wt_hbm, wt),
+    ]
+    loads = [pltpu.make_async_copy(src, dst, weight_sem.at[i]) for i, (src, dst) in enumerate(places)]
+    for load in loads:
+        load.start()
+    members = group_matrix()
+    for load in loads[:2]:
+        load.wait()
 
     count = counts[0, tm]
-    g16 = g_ref[...]
-    g = g16.astype(F32)
+    g = g_ref[...].astype(F32)
     g_frames = [frame_of(g, s) for s in range(CAP)]
     last = jnp.where(count == 3, g_frames[2], jnp.where(count == 2, g_frames[1], g_frames[0]))
     edge[0] = g_frames[0].astype(BF16)
     edge[1] = last.astype(BF16)
-    pl.semaphore_wait(barrier, len(peers))
     halo_copies = [
         remote(edge.at[0], halo.at[1], halo_send.at[0], halo_recv.at[1], (dp, before)),
         remote(edge.at[1], halo.at[0], halo_send.at[1], halo_recv.at[0], (dp, after)),
     ]
-    for copy in halo_copies:
-        copy.start()
-
-    members = group_matrix()
-    gain, shift = gain_ref[...], shift_ref[...]
+    for load in loads[2:5]:
+        load.wait()
+
+    gain, shift = gain_ref[...].reshape(1, CH), shift_ref[...].reshape(1, CH)
     x = x_ref[...].astype(F32)
     x_frames = [frame_of(x, s) for s in range(CAP)]
     means = group_means([column_sum(v) for v in x_frames], members)
@@ -282,7 +285,10 @@
     padded[...] = jnp.zeros_like(padded)
     stage_shifts(normed * sig_n, line, padded)
 
-    load_s.wait()
+    pl.semaphore_wait(barrier, len(peers))
+    for copy in halo_copies:
+        copy.start()
+    loads[5].wait()
     mixed = jnp.zeros((ROWS, CH), F32)
     for tap in range(9):
         mixed = mixed + dot(shifted(padded, tap % 3, tap // 3), ws[:, tap * CH : (tap + 1) * CH], 1, 1)
@@ -296,23 +302,30 @@
         copy.wait()
     prev_edge = jnp.where(tm == 0, 0.0, halo[0].astype(F32))
     next_edge = jnp.where(tm == 7, 0.0, halo[1].astype(F32))
-    g_prev = jnp.concatenate([prev_edge, g_frames[0], g_frames[1]], axis=0).astype(BF16)
-    g_next = jnp.concatenate(
+    g_ext = jnp.concatenate(
         [
+            prev_edge,
+            g_frames[0],
             jnp.where(count == 1, next_edge, g_frames[1]),
             jnp.where(count == 2, next_edge, g_frames[2]),
             next_edge,
         ],
         axis=0,
-    ).astype(BF16)
-    taps = (g_next, g16, g_prev)
-
+    )
+
+    g_turned = g_ext.T.astype(BF16)
+    g_ext = g_ext.astype(BF16)
     none = jnp.zeros((ROWS, 64), BF16)
     u_low = jnp.concatenate([u, none], axis=1)
     u_high = jnp.concatenate([none, u], axis=1)
-    t0 = dot(taps[0], u_low, 0, 0)
-    t1 = dot(taps[1], u_high, 0, 0)
-    t2 = dot(taps[2], u_low, 0, 0)
+
+    def below(value, frames):
+        zero = jnp.zeros((PIX, value.shape[1]), BF16)
+        return jnp.concatenate([zero] * frames + [value] + [zero] * (2 - frames), axis=0)
+
+    t0 = dot(g_turned, below(u_low, 2), 1, 0)
+    t1 = dot(g_turned, below(u_high, 1), 1, 0)
+    t2 = dot(g_turned, below(u_low, 0), 1, 0)
     units = [
         t0[:, 0:128], t0[:, 128:256], t0[:, 256:384] + t1[:, 0:128], t1[:, 128:256], t1[:, 256:384],
         t2[:, 0:128], t2[:, 128:256], t2[:, 256:384],
@@ -323,44 +336,56 @@
             part[r * UNITS + l] = piece
             part16[r * UNITS + l] = piece.astype(BF16)
 
-    core_copy = remote(part16.at[pl.ds((1 - core) * 16, 16)], from_core, core_sem.at[0], core_sem.at[1], partner)
-    core_copy.start()
-
-    load_t.wait()
+    groups = plane + [chip]
+    core_copies = [
+        remote(
+            part16.at[pl.ds((1 - core) * 16 + p * 4, 4)], from_core.at[pl.ds(p * 4, 4)],
+            core_send.at[j], core_recv.at[j], partner,
+        )
+        for j, p in enumerate(groups)
+    ]
+    for copy in core_copies:
+        copy.start()
+
+    loads[6].wait()
     du = jnp.zeros((ROWS, CH), F32)
     for k in range(3):
-        du = du + dot(taps[k], wt[:, k * CH : (k + 1) * CH], 1, 0)
+        du = du + dot(g_ext[(2 - k) * PIX : (2 - k) * PIX + ROWS], wt[:, k * CH : (k + 1) * CH], 1, 0)
     back_t = (sig_y * (1.0 + y * (1.0 - sig_y)) * du).astype(BF16).astype(F32)
     dy = jnp.where(live, (g + back_t).astype(BF16).astype(F32), 0.0)
 
-    core_copy.wait()
-    quad = part[pl.ds(core * 16, 16)] + from_core[...].astype(F32)
-    part[pl.ds(core * 16, 16)] = quad
-    quad16[...] = quad.astype(BF16)
-    plane_copies = [
-        remote(quad16.at[pl.ds(p * 4, 4)], from_plane.at[d], plane_send.at[d], plane_recv.at[d], at(dp, p, core))
-        for d, p in enumerate(plane)
-    ]
-    for copy in plane_copies:
-        copy.start()
+    z_order = z_to + [dp]
+    plane_copies = []
+    for j, p in enumerate(groups):
+        core_copies[j].wait()
+        quad = part[pl.ds(core * 16 + p * 4, 4)] + from_core[pl.ds(p * 4, 4)].astype(F32)
+        if j == 3:
+            own[...] = quad
+            continue
+        quad16[j] = quad.astype(BF16)
+        for k, z in enumerate(z_order):
+            i = j * 4 + k
+            copy = remote(quad16.at[j, z], from_plane.at[j, k], plane_send.at[i], plane_recv.at[i], at(dp, p, core))
+            copy.start()
+            plane_copies.append(copy)
 
     stage_shifts(dy, line, padded)
     da = jnp.zeros((ROWS, CH), F32)
     for tap in range(9):
         da = da + dot(shifted(padded, 2 - tap % 3, 2 - tap // 3), ws[:, tap * CH : (tap + 1) * CH], 1, 0)
 
-    for copy in plane_copies:
-        copy.wait()
-    first = core * 16 + chip * 4
-    four = part[pl.ds(first, 4)] + from_plane[0].astype(F32) + from_plane[1].astype(F32) + from_plane[2].astype(F32)
-    part[pl.ds(first, 4)] = four
-    own16[...] = four.astype(BF16)
-    z_copies = [
-        remote(own16.at[z], from_z.at[d], z_send.at[d], z_recv.at[d], at(z, chip, core))
-        for d, z in enumerate(z_to)
-    ]
-    for copy in z_copies:
+    z_copies = []
+    for k, z in enumerate(z_order):
+        for j in range(3):
+            plane_copies[j * 4 + k].wait()
+        four = own[z] + from_plane[0, k].astype(F32) + from_plane[1, k].astype(F32) + from_plane[2, k].astype(F32)
+        if k == 3:
+            total = four
+            continue
+        own16[k] = four.astype(BF16)
+        copy = remote(own16.at[k], from_z.at[k], z_send.at[k], z_recv.at[k], at(z, chip, core))
         copy.start()
+        z_copies.append(copy)
 
     dhat = da * (sig_n * (1.0 + normed * (1.0 - sig_n))) * gain
     dhat_frames = [frame_of(dhat, s) for s in range(CAP)]
@@ -378,8 +403,9 @@
 
     for copy in z_copies:
         copy.wait()
+    first = core * 16 + chip * 4
     mine = first + dp
-    total = part[mine] + from_z[0].astype(F32) + from_z[1].astype(F32) + from_z[2].astype(F32)
+    total = total + from_z[0].astype(F32) + from_z[1].astype(F32) + from_z[2].astype(F32)
     full[mine] = total.astype(BF16)
 
     sent = []
@@ -426,7 +452,7 @@
 
 def fused_shards(frames_in, cotangent, counts, norm_gain, norm_shift, spatial_weight, temporal_weight):
     vmem = pl.BlockSpec(memory_space=pltpu.VMEM)
-    hbm = pl.BlockSpec(memory_space=pl.ANY)
+    hbm = pl.BlockSpec(memory_space=pltpu.HBM)
     dma = pltpu.SemaphoreType.DMA
     out, grad = pl.pallas_call(
         fused_kernel,
@@ -434,9 +460,14 @@
             jax.ShapeDtypeStruct((ROWS, CH), BF16),
             jax.ShapeDtypeStruct((CH, 3 * CH), F32),
         ),
-        in_specs=[pl.BlockSpec(memory_space=pltpu.SMEM), vmem, vmem, vmem, vmem, hbm, hbm],
+        in_specs=[hbm] * 7,
         out_specs=(vmem, vmem),
         scratch_shapes=[
+            pltpu.SMEM((1, 8), jnp.int32),
+            pltpu.VMEM((ROWS, CH), BF16),
+            pltpu.VMEM((ROWS, CH), BF16),
+            pltpu.VMEM((CH,), F32),
+            pltpu.VMEM((CH,), F32),
             pltpu.VMEM((CH, 9 * CH), BF16),
             pltpu.VMEM((CH, 3 * CH), BF16),
             pltpu.VMEM((ROWS + 16, CH), F32),
@@ -446,23 +477,24 @@
             pltpu.VMEM((CHUNKS, BLOCK, LANE), F32),
             pltpu.VMEM((CHUNKS, BLOCK, LANE), BF16),
             pltpu.VMEM((16, BLOCK, LANE), BF16),
-            pltpu.VMEM((16, BLOCK, LANE), BF16),
             pltpu.VMEM((3, 4, BLOCK, LANE), BF16),
-            pltpu.VMEM((4, BLOCK, LANE), BF16),
+            pltpu.VMEM((3, 4, BLOCK, LANE), BF16),
+            pltpu.VMEM((4, BLOCK, LANE), F32),
+            pltpu.VMEM((3, BLOCK, LANE), BF16),
             pltpu.VMEM((3, BLOCK, LANE), BF16),
             pltpu.VMEM((CHUNKS, BLOCK, LANE), BF16),
-            dma((2,)), dma((2,)), dma((2,)), dma((2,)), dma((3,)), dma((3,)), dma((3,)), dma((3,)),
+            dma((7,)), dma((2,)), dma((2,)), dma((4,)), dma((4,)), dma((12,)), dma((12,)), dma((3,)), dma((3,)),
             dma((31,)), dma((3,)), dma((12,)), dma((16,)),
         ],
         compiler_params=pltpu.CompilerParams(
-            collective_id=0, has_side_effects=True, vmem_limit_bytes=40 * 1024 * 1024
+            collective_id=0, has_side_effects=True, vmem_limit_bytes=60 * 1024 * 1024
         ),
     )(
         counts,
         frames_in.reshape(ROWS, CH),
         cotangent.reshape(ROWS, CH),
-        norm_gain.reshape(1, CH),
-        norm_shift.reshape(1, CH),
+        norm_gain,
+        norm_shift,
         spatial_weight.T,
         temporal_weight.T,
     )

time: 40.6 us -> 35.7 us (0.88)
  local copies, waits for them, and re-layouts: 8.16 us -> 4.11 us
  Pallas kernels: 31.5 us -> 30.7 us
    unnamed x12 -> x2, local copies, waits for them, and re-layouts: 6.8 us -> 4.11 us
    reshape x2 -> x0, local copies, waits for them, and re-layouts: 1.37 us -> none  [the longest x1 0.68 us: fused_shards(): norm_gain.reshape(1, CH)]
    pallas_call x1, Pallas kernels: 31.5 us -> 30.7 us  [fused_shards(): pl.pallas_call(fused_kernel, out_shape=(jax.ShapeDtypeStruct((ROWS, CH),...]
where the time goes in v2:
time: 35.7 us; the launch traced here: 35.5 us
  Pallas kernels  30.7 us (86%)
  local copies, waits for them, and re-layouts  4.11 us (12%)
  between operations  0.64 us (2%)
    pallas_call x1, Pallas kernels, fused_shards(): pl.pallas_call(fused_kernel, out_shape=(jax.ShapeDtypeStruct((ROWS, CH),...  30.7 us
    unnamed x2, local copies, waits for them, and re-layouts  4.11 us

profile of v2, /device:TPU:0, one launch (start us, length us, event | category | flops | bytes accessed | tf_op | source)
XLA Modules:
  0.0 35.5 jit_solution(9359652929549967313)
XLA Ops:
  0.6 30.7 %shard_map.86 = (bf16[192,320]{1,0:T(8,128)(2,1)}, f32[320,960]{1,0:T(8,128)}) custom-call(s32[1,8]{1,0:T(1,128)} %counts_hbm.1, bf16[192,320]{1,0:T(8,128)(2,1)} %bitcast.9, bf16[192,320]{1,0:T(8,128)(2,1)} %bitcast.10, f32[320]{0:T(512)} %gain_hbm.1, f32[320]{0:T(512)} %shift_hbm.1, bf16[320,2880]{1,0:T(8,128)(2,1)} %bitcast.6, bf16[320,960]{1,0:T(8,128)(2,1)} %bitcast.8), custom_call_target="tpu_custom_call" | custom-call | tf_op jit(solution)/shard_map/pallas_call | solution.py:457
  31.4 1.6 %copy.11 = bf16[1,3,8,8,320]{4,3,2,1,0:T(8,128)(2,1)} copy(bf16[1,3,8,8,320]{4,3,2,1,0:T(8,128)(2,1)} %bitcast.11) | data formatting | bytes 245760
  33.0 2.5 %copy.12 = f32[960,320]{0,1:T(8,128)} copy(f32[960,320]{0,1:T(8,128)} %bitcast.7) | data formatting | bytes 2457600

commit v3 on v2

--- a/solution.py
+++ b/solution.py
@@ -213,6 +213,20 @@
         padded[j, :, 1 : 1 + SIDE] = moved.reshape(CAP, SIDE, SIDE, CH)
 
 
+def turned_patches(value):
+    wide = jnp.concatenate([value, jnp.zeros((64, CH), F32)], axis=0).T
+    pixel = lax.broadcasted_iota(jnp.int32, wide.shape, 1)
+    row, column = (pixel // SIDE) % SIDE, pixel % SIDE
+    pieces = []
+    for i in (-1, 0, 1):
+        for j in (-1, 0, 1):
+            move = (-(i * SIDE + j)) % wide.shape[1]
+            moved = pltpu.roll(wide, move, 1) if move else wide
+            inside = (row + i >= 0) & (row + i < SIDE) & (column + j >= 0) & (column + j < SIDE)
+            pieces.append(jnp.where(inside, moved, 0.0).astype(BF16))
+    return jnp.concatenate(pieces, axis=0)
+
+
 def shifted(padded, j, i):
     return padded[j, :, i : i + SIDE].reshape(ROWS, CH).astype(BF16)
 
@@ -232,11 +246,11 @@
         return (z, chip_id * 2 + core_id)
 
     plane = [yy * 2 + (1 - xx), (1 - yy) * 2 + xx, (1 - yy) * 2 + (1 - xx)]
-    z_to = [lax.rem(dp + d, 4) for d in (1, 2, 3)]
-    z_from = [lax.rem(dp + 4 - d, 4) for d in (1, 2, 3)]
+    near = [dp + 1 - 2 * (dp % 2), 2 - dp // 2, 3 - 3 * (dp // 2)]
+    far = near[::-1]
     before, after = lax.rem(tm + 7, 8), lax.rem(tm + 1, 8)
     partner = at(dp, chip, 1 - core)
-    peers = [(dp, before), (dp, after)] + [at(dp, p, core) for p in plane] + [at(z, chip, core) for z in z_to]
+    peers = [(dp, before), (dp, after)] + [at(dp, p, core) for p in plane] + [at(z, chip, core) for z in near]
 
     def remote(src, dst, send_sem, recv_sem, device):
         copy = pltpu.make_async_remote_copy(
@@ -283,15 +297,12 @@
     normed = xhat * gain + shift
     sig_n = sigmoid(normed)
     padded[...] = jnp.zeros_like(padded)
-    stage_shifts(normed * sig_n, line, padded)
-
     pl.semaphore_wait(barrier, len(peers))
     for copy in halo_copies:
         copy.start()
+    patched = turned_patches(normed * sig_n)
     loads[5].wait()
-    mixed = jnp.zeros((ROWS, CH), F32)
-    for tap in range(9):
-        mixed = mixed + dot(shifted(padded, tap % 3, tap // 3), ws[:, tap * CH : (tap + 1) * CH], 1, 1)
+    mixed = dot(ws[...], patched, 1, 0).T[:ROWS]
     y = (x + mixed).astype(BF16).astype(F32)
     sig_y = sigmoid(y)
     slot = lax.broadcasted_iota(jnp.int32, (ROWS, CH), 0) // PIX
@@ -354,38 +365,42 @@
     back_t = (sig_y * (1.0 + y * (1.0 - sig_y)) * du).astype(BF16).astype(F32)
     dy = jnp.where(live, (g + back_t).astype(BF16).astype(F32), 0.0)
 
-    z_order = z_to + [dp]
-    plane_copies = []
+    z_order = far + [dp]
     for j, p in enumerate(groups):
         core_copies[j].wait()
         quad = part[pl.ds(core * 16 + p * 4, 4)] + from_core[pl.ds(p * 4, 4)].astype(F32)
         if j == 3:
             own[...] = quad
-            continue
-        quad16[j] = quad.astype(BF16)
-        for k, z in enumerate(z_order):
-            i = j * 4 + k
+        else:
+            quad16[j] = quad.astype(BF16)
+    plane_copies = []
+    for k, z in enumerate(z_order):
+        for j, p in enumerate(plane):
+            i = k * 3 + j
             copy = remote(quad16.at[j, z], from_plane.at[j, k], plane_send.at[i], plane_recv.at[i], at(dp, p, core))
             copy.start()
             plane_copies.append(copy)
+
+    def summed_plane(k, z):
+        for j in range(3):
+            plane_copies[k * 3 + j].wait()
+        return own[z] + from_plane[0, k].astype(F32) + from_plane[1, k].astype(F32) + from_plane[2, k].astype(F32)
+
+    z_copies = []
+
+    def pass_to_z(k):
+        own16[k] = summed_plane(k, z_order[k]).astype(BF16)
+        copy = remote(own16.at[k], from_z.at[dp], z_send.at[k], z_recv.at[dp], at(z_order[k], chip, core))
+        copy.start()
+        z_copies.append(copy)
 
     stage_shifts(dy, line, padded)
     da = jnp.zeros((ROWS, CH), F32)
     for tap in range(9):
         da = da + dot(shifted(padded, 2 - tap % 3, 2 - tap // 3), ws[:, tap * CH : (tap + 1) * CH], 1, 0)
-
-    z_copies = []
-    for k, z in enumerate(z_order):
-        for j in range(3):
-            plane_copies[j * 4 + k].wait()
-        four = own[z] + from_plane[0, k].astype(F32) + from_plane[1, k].astype(F32) + from_plane[2, k].astype(F32)
-        if k == 3:
-            total = four
-            continue
-        own16[k] = four.astype(BF16)
-        copy = remote(own16.at[k], from_z.at[k], z_send.at[k], z_recv.at[k], at(z, chip, core))
-        copy.start()
-        z_copies.append(copy)
+        if tap in (4, 6, 8):
+            pass_to_z(tap // 2 - 2)
+    total = summed_plane(3, dp)
 
     dhat = da * (sig_n * (1.0 + normed * (1.0 - sig_n))) * gain
     dhat_frames = [frame_of(dhat, s) for s in range(CAP)]
@@ -401,53 +416,56 @@
     )
     out_ref[...] = jnp.where(live, dy + dx, 0.0).astype(BF16)
 
-    for copy in z_copies:
-        copy.wait()
     first = core * 16 + chip * 4
     mine = first + dp
-    total = total + from_z[0].astype(F32) + from_z[1].astype(F32) + from_z[2].astype(F32)
+    for z in near:
+        remote(from_z.at[z], from_z.at[z], z_send.at[0], z_recv.at[z], partner).wait_recv()
+        total = total + from_z[z].astype(F32)
     full[mine] = total.astype(BF16)
 
     sent = []
 
-    def pass_on(chunk, sem_id, device, recv_sem):
-        copy = remote(full.at[chunk], full.at[chunk], gather_send.at[sem_id], recv_sem, device)
+    def pass_on(chunk, device, recv_sem):
+        copy = remote(full.at[chunk], full.at[chunk], gather_send.at[len(sent)], recv_sem, device)
         copy.start()
         sent.append(copy)
 
-    for d, z in enumerate(z_to):
-        pass_on(mine, d, at(z, chip, core), gather_z.at[d])
-    for d, p in enumerate(plane):
-        pass_on(mine, 3 + d, at(dp, p, core), gather_plane.at[d])
-    pass_on(mine, 6, partner, gather_core.at[0])
-    for k, z in enumerate(z_from):
-        chunk = first + z
-        remote(full.at[chunk], full.at[chunk], gather_send.at[0], gather_z.at[k], partner).wait_recv()
-        for d, p in enumerate(plane):
-            pass_on(chunk, 7 + k * 4 + d, at(dp, p, core), gather_plane.at[(k + 1) * 3 + d])
-        pass_on(chunk, 7 + k * 4 + 3, partner, gather_core.at[k + 1])
-    sem_id = 19
-    for k, z in enumerate([dp] + z_from):
-        for d, p in enumerate(plane):
+    def await_chunk(chunk, recv_sem):
+        remote(full.at[chunk], full.at[chunk], gather_send.at[0], recv_sem, partner).wait_recv()
+
+    for z in far:
+        pass_on(mine, at(z, chip, core), gather_z.at[dp])
+    for j, p in enumerate(plane):
+        pass_on(mine, at(dp, p, core), gather_plane.at[dp * 3 + j])
+    pass_on(mine, partner, gather_core.at[dp * 4 + 3])
+    for z in near:
+        await_chunk(first + z, gather_z.at[z])
+        for j, p in enumerate(plane):
+            pass_on(first + z, at(dp, p, core), gather_plane.at[z * 3 + j])
+        pass_on(first + z, partner, gather_core.at[z * 4 + 3])
+    for z in [dp] + near:
+        for j, p in enumerate(plane):
             chunk = core * 16 + p * 4 + z
-            remote(full.at[chunk], full.at[chunk], gather_send.at[0], gather_plane.at[k * 3 + d], partner).wait_recv()
-            pass_on(chunk, sem_id, partner, gather_core.at[4 + k * 3 + d])
-            sem_id = sem_id + 1
-    others = [chip] + plane
-    for k, z in enumerate([dp] + z_from):
-        for d, p in enumerate(others):
-            chunk = (1 - core) * 16 + p * 4 + z
-            slot_id = k if d == 0 else 4 + k * 3 + d - 1
-            remote(full.at[chunk], full.at[chunk], gather_send.at[0], gather_core.at[slot_id], partner).wait_recv()
-    for copy in sent:
+            await_chunk(chunk, gather_plane.at[z * 3 + j])
+            pass_on(chunk, partner, gather_core.at[z * 4 + j])
+
+    scale = 1.0 / math.sqrt(4 * 2 * 8 * PIX)
+
+    def put(half):
+        for r in range(2):
+            rows = pl.ds(pl.multiple_of(half * 2 * BLOCK + r * BLOCK, 8), BLOCK)
+            for l in range(UNITS):
+                width = min(LANE, 3 * CH - l * LANE)
+                value = full[half * 16 + r * UNITS + l].astype(F32) * scale
+                grad_ref[rows, l * LANE : l * LANE + width] = value[:, :width]
+
+    put(core)
+    for z in [dp] + near:
+        for j, p in enumerate(groups):
+            await_chunk((1 - core) * 16 + p * 4 + z, gather_core.at[z * 4 + j])
+    put(1 - core)
+    for copy in z_copies + sent:
         copy.wait_send()
-
-    scale = 1.0 / math.sqrt(4 * 2 * 8 * PIX)
-    for r in range(4):
-        for l in range(UNITS):
-            width = min(LANE, 3 * CH - l * LANE)
-            value = full[r * UNITS + l].astype(F32) * scale
-            grad_ref[r * BLOCK : (r + 1) * BLOCK, l * LANE : l * LANE + width] = value[:, :width]
 
 
 def fused_shards(frames_in, cotangent, counts, norm_gain, norm_shift, spatial_weight, temporal_weight):
@@ -457,8 +475,8 @@
     out, grad = pl.pallas_call(
         fused_kernel,
         out_shape=(
-            jax.ShapeDtypeStruct((ROWS, CH), BF16),
-            jax.ShapeDtypeStruct((CH, 3 * CH), F32),
+            pltpu.VMEM((ROWS, CH), BF16),
+            pltpu.VMEM((CH, 3 * CH), F32),
         ),
         in_specs=[hbm] * 7,
         out_specs=(vmem, vmem),
@@ -481,10 +499,10 @@
             pltpu.VMEM((3, 4, BLOCK, LANE), BF16),
             pltpu.VMEM((4, BLOCK, LANE), F32),
             pltpu.VMEM((3, BLOCK, LANE), BF16),
-            pltpu.VMEM((3, BLOCK, LANE), BF16),
+            pltpu.VMEM((4, BLOCK, LANE), BF16),
             pltpu.VMEM((CHUNKS, BLOCK, LANE), BF16),
-            dma((7,)), dma((2,)), dma((2,)), dma((4,)), dma((4,)), dma((12,)), dma((12,)), dma((3,)), dma((3,)),
-            dma((31,)), dma((3,)), dma((12,)), dma((16,)),
+            dma((7,)), dma((2,)), dma((2,)), dma((4,)), dma((4,)), dma((12,)), dma((12,)), dma((3,)), dma((4,)),
+            dma((31,)), dma((4,)), dma((12,)), dma((16,)),
         ],
         compiler_params=pltpu.CompilerParams(
             collective_id=0, has_side_effects=True, vmem_limit_bytes=60 * 1024 * 1024

time: 35.7 us -> 31.5 us (0.88)
  local copies, waits for them, and re-layouts: 4.11 us -> 1.72 us
  Pallas kernels: 30.7 us -> 29 us
    unnamed x2, local copies, waits for them, and re-layouts: 4.11 us -> 1.72 us
    pallas_call x1, Pallas kernels: 30.7 us -> 29 us  [fused_shards(): pl.pallas_call(fused_kernel, out_shape=(pltpu.VMEM((ROWS, CH), BF16), plt...]
where the time goes in v3:
time: 31.5 us; the launch traced here: 31.4 us
  Pallas kernels  29 us (92%)
  local copies, waits for them, and re-layouts  1.72 us (5%)
  between operations  0.64 us (2%)
    pallas_call x1, Pallas kernels, fused_shards(): pl.pallas_call(fused_kernel, out_shape=(pltpu.VMEM((ROWS, CH), BF16), plt...  29 us
    unnamed x2, local copies, waits for them, and re-layouts  1.72 us

profile of v3, /device:TPU:0, one launch (start us, length us, event | category | flops | bytes accessed | tf_op | source)
XLA Modules:
  0.0 31.4 jit_solution(11398410990158571240)
XLA Ops:
  0.6 29.0 %shard_map.86 = (bf16[192,320]{1,0:T(8,128)(2,1)S(1)}, f32[320,960]{1,0:T(8,128)S(1)}) custom-call(s32[1,8]{1,0:T(1,128)} %counts_hbm.1, bf16[192,320]{1,0:T(8,128)(2,1)} %bitcast.10, bf16[192,320]{1,0:T(8,128)(2,1)} %bitcast.11, f32[320]{0:T(512)} %gain_hbm.1, f32[320]{0:T(512)} %shift_hbm.1, bf16[320,2880]{1,0:T(8,128)(2,1)} %bitcast.8, ...), custom_call_target="tpu_custom_call" | custom-call | tf_op jit(solution)/shard_map/pallas_call | solution.py:475
  29.6 0.7 %copy.11 = bf16[1,3,8,8,320]{4,3,2,1,0:T(8,128)(2,1)} copy(bf16[1,3,8,8,320]{4,3,2,1,0:T(8,128)(2,1)S(1)} %bitcast.7) | data formatting | bytes 245760
  30.3 1.1 %copy.12 = f32[960,320]{0,1:T(8,128)} copy(f32[960,320]{0,1:T(8,128)S(1)} %bitcast.6) | data formatting | bytes 2457600

commit v4 on v3

--- a/solution.py
+++ b/solution.py
@@ -205,7 +205,7 @@
 
 
 def stage_shifts(value, line, padded):
-    column = lax.broadcasted_iota(jnp.int32, (ROWS, CH), 0) % SIDE
+    column = lax.broadcasted_iota(jnp.int32, (ROWS, CH), 0) & (SIDE - 1)
     line[8 : 8 + ROWS, :] = value
     left = jnp.where(column == 0, 0.0, line[7 : 7 + ROWS, :])
     right = jnp.where(column == SIDE - 1, 0.0, line[9 : 9 + ROWS, :])
@@ -215,15 +215,15 @@
 
 def turned_patches(value):
     wide = jnp.concatenate([value, jnp.zeros((64, CH), F32)], axis=0).T
-    pixel = lax.broadcasted_iota(jnp.int32, wide.shape, 1)
-    row, column = (pixel // SIDE) % SIDE, pixel % SIDE
+    pixel = lax.broadcasted_iota(jnp.int32, (1, wide.shape[1]), 1)
+    row, column = (pixel & (PIX - 1)) >> 3, pixel & (SIDE - 1)
     pieces = []
     for i in (-1, 0, 1):
         for j in (-1, 0, 1):
             move = (-(i * SIDE + j)) % wide.shape[1]
             moved = pltpu.roll(wide, move, 1) if move else wide
             inside = (row + i >= 0) & (row + i < SIDE) & (column + j >= 0) & (column + j < SIDE)
-            pieces.append(jnp.where(inside, moved, 0.0).astype(BF16))
+            pieces.append((moved * inside.astype(F32)).astype(BF16))
     return jnp.concatenate(pieces, axis=0)
 
 
@@ -233,7 +233,7 @@
 
 def fused_kernel(
     counts_hbm, x_hbm, g_hbm, gain_hbm, shift_hbm, ws_hbm, wt_hbm, out_ref, grad_ref,
-    counts, x_ref, g_ref, gain_ref, shift_ref, ws, wt, line, padded, edge, halo, part, part16, from_core, quad16, from_plane, own, own16, from_z, full,
+    counts, x_ref, g_ref, gain_ref, shift_ref, ws, wt, line, padded, edge, halo, turned, part, part16, from_core, quad16, from_plane, own, own16, from_z, full,
     weight_sem, halo_send, halo_recv, core_send, core_recv, plane_send, plane_recv, z_send, z_recv,
     gather_send, gather_z, gather_plane, gather_core,
 ):
@@ -283,6 +283,9 @@
         remote(edge.at[0], halo.at[1], halo_send.at[0], halo_recv.at[1], (dp, before)),
         remote(edge.at[1], halo.at[0], halo_send.at[1], halo_recv.at[0], (dp, after)),
     ]
+    pl.semaphore_wait(barrier, len(peers))
+    for copy in halo_copies:
+        copy.start()
     for load in loads[2:5]:
         load.wait()
 
@@ -297,18 +300,7 @@
     normed = xhat * gain + shift
     sig_n = sigmoid(normed)
     padded[...] = jnp.zeros_like(padded)
-    pl.semaphore_wait(barrier, len(peers))
-    for copy in halo_copies:
-        copy.start()
     patched = turned_patches(normed * sig_n)
-    loads[5].wait()
-    mixed = dot(ws[...], patched, 1, 0).T[:ROWS]
-    y = (x + mixed).astype(BF16).astype(F32)
-    sig_y = sigmoid(y)
-    slot = lax.broadcasted_iota(jnp.int32, (ROWS, CH), 0) // PIX
-    live = slot < count
-    u = jnp.where(live, y * sig_y, 0.0).astype(BF16)
-
     for copy in halo_copies:
         copy.wait()
     prev_edge = jnp.where(tm == 0, 0.0, halo[0].astype(F32))
@@ -323,9 +315,16 @@
         ],
         axis=0,
     )
-
-    g_turned = g_ext.T.astype(BF16)
+    turned[...] = g_ext.T.astype(BF16)
     g_ext = g_ext.astype(BF16)
+
+    loads[5].wait()
+    mixed = dot(ws[...], patched, 1, 0).T[:ROWS]
+    y = (x + mixed).astype(BF16).astype(F32)
+    sig_y = sigmoid(y)
+    live = lax.broadcasted_iota(jnp.int32, (ROWS, CH), 0) < count * PIX
+    u = jnp.where(live, y * sig_y, 0.0).astype(BF16)
+
     none = jnp.zeros((ROWS, 64), BF16)
     u_low = jnp.concatenate([u, none], axis=1)
     u_high = jnp.concatenate([none, u], axis=1)
@@ -334,29 +333,31 @@
         zero = jnp.zeros((PIX, value.shape[1]), BF16)
         return jnp.concatenate([zero] * frames + [value] + [zero] * (2 - frames), axis=0)
 
-    t0 = dot(g_turned, below(u_low, 2), 1, 0)
-    t1 = dot(g_turned, below(u_high, 1), 1, 0)
-    t2 = dot(g_turned, below(u_low, 0), 1, 0)
-    units = [
-        t0[:, 0:128], t0[:, 128:256], t0[:, 256:384] + t1[:, 0:128], t1[:, 128:256], t1[:, 256:384],
-        t2[:, 0:128], t2[:, 128:256], t2[:, 256:384],
-    ]
-    for r in range(4):
-        for l in range(UNITS):
-            piece = units[l][r * BLOCK : (r + 1) * BLOCK]
-            part[r * UNITS + l] = piece
-            part16[r * UNITS + l] = piece.astype(BF16)
-
+    first_tap, second_tap, third_tap = below(u_low, 2), below(u_high, 1), below(u_low, 0)
+
+    def gradient_half(half):
+        rows = turned[pl.ds(pl.multiple_of(half * 2 * BLOCK, 16), 2 * BLOCK), :]
+        t0, t1, t2 = dot(rows, first_tap, 1, 0), dot(rows, second_tap, 1, 0), dot(rows, third_tap, 1, 0)
+        units = [
+            t0[:, 0:128], t0[:, 128:256], t0[:, 256:384] + t1[:, 0:128], t1[:, 128:256], t1[:, 256:384],
+            t2[:, 0:128], t2[:, 128:256], t2[:, 256:384],
+        ]
+        return [(r * UNITS + l, units[l][r * BLOCK : (r + 1) * BLOCK]) for r in range(2) for l in range(UNITS)]
+
+    for i, piece in gradient_half(1 - core):
+        part16[i] = piece.astype(BF16)
     groups = plane + [chip]
     core_copies = [
         remote(
-            part16.at[pl.ds((1 - core) * 16 + p * 4, 4)], from_core.at[pl.ds(p * 4, 4)],
+            part16.at[pl.ds(p * 4, 4)], from_core.at[pl.ds(p * 4, 4)],
             core_send.at[j], core_recv.at[j], partner,
         )
         for j, p in enumerate(groups)
     ]
     for copy in core_copies:
         copy.start()
+    for i, piece in gradient_half(core):
+        part[i] = piece
 
     loads[6].wait()
     du = jnp.zeros((ROWS, CH), F32)
@@ -368,7 +369,7 @@
     z_order = far + [dp]
     for j, p in enumerate(groups):
         core_copies[j].wait()
-        quad = part[pl.ds(core * 16 + p * 4, 4)] + from_core[pl.ds(p * 4, 4)].astype(F32)
+        quad = part[pl.ds(p * 4, 4)] + from_core[pl.ds(p * 4, 4)].astype(F32)
         if j == 3:
             own[...] = quad
         else:
@@ -492,8 +493,9 @@
             pltpu.VMEM((3, CAP, SIDE + 2, SIDE, CH), F32),
             pltpu.VMEM((2, PIX, CH), BF16),
             pltpu.VMEM((2, PIX, CH), BF16),
-            pltpu.VMEM((CHUNKS, BLOCK, LANE), F32),
-            pltpu.VMEM((CHUNKS, BLOCK, LANE), BF16),
+            pltpu.VMEM((CH, (CAP + 2) * PIX), BF16),
+            pltpu.VMEM((16, BLOCK, LANE), F32),
+            pltpu.VMEM((16, BLOCK, LANE), BF16),
             pltpu.VMEM((16, BLOCK, LANE), BF16),
             pltpu.VMEM((3, 4, BLOCK, LANE), BF16),
             pltpu.VMEM((3, 4, BLOCK, LANE), BF16),

time: 31.5 us -> 31.9 us (1.013)
  Pallas kernels: 29 us -> 29.4 us
    pallas_call x1, Pallas kernels: 29 us -> 29.4 us  [fused_shards(): pl.pallas_call(fused_kernel, out_shape=(pltpu.VMEM((ROWS, CH), BF16), plt...]
where the time goes in v4:
time: 31.9 us; the launch traced here: 31.7 us
  Pallas kernels  29.4 us (92%)
  local copies, waits for them, and re-layouts  1.72 us (5%)
  between operations  0.64 us (2%)
    pallas_call x1, Pallas kernels, fused_shards(): pl.pallas_call(fused_kernel, out_shape=(pltpu.VMEM((ROWS, CH), BF16), plt...  29.4 us
    unnamed x2, local copies, waits for them, and re-layouts  1.72 us

profile of v4, /device:TPU:0, one launch (start us, length us, event | category | flops | bytes accessed | tf_op | source)
XLA Modules:
  0.0 31.7 jit_solution(6042888469743418947)
XLA Ops:
  0.6 29.4 %shard_map.86 = (bf16[192,320]{1,0:T(8,128)(2,1)S(1)}, f32[320,960]{1,0:T(8,128)S(1)}) custom-call(s32[1,8]{1,0:T(1,128)} %counts_hbm.1, bf16[192,320]{1,0:T(8,128)(2,1)} %bitcast.10, bf16[192,320]{1,0:T(8,128)(2,1)} %bitcast.11, f32[320]{0:T(512)} %gain_hbm.1, f32[320]{0:T(512)} %shift_hbm.1, bf16[320,2880]{1,0:T(8,128)(2,1)} %bitcast.8, ...), custom_call_target="tpu_custom_call" | custom-call | tf_op jit(solution)/shard_map/pallas_call | solution.py:476
  30.0 0.7 %copy.11 = bf16[1,3,8,8,320]{4,3,2,1,0:T(8,128)(2,1)} copy(bf16[1,3,8,8,320]{4,3,2,1,0:T(8,128)(2,1)S(1)} %bitcast.7) | data formatting | bytes 245760
  30.7 1.1 %copy.12 = f32[960,320]{0,1:T(8,128)} copy(f32[960,320]{0,1:T(8,128)S(1)} %bitcast.6) | data formatting | bytes 2457600

commit v5 on v4

--- a/solution.py
+++ b/solution.py
@@ -233,7 +233,7 @@
 
 def fused_kernel(
     counts_hbm, x_hbm, g_hbm, gain_hbm, shift_hbm, ws_hbm, wt_hbm, out_ref, grad_ref,
-    counts, x_ref, g_ref, gain_ref, shift_ref, ws, wt, line, padded, edge, halo, turned, part, part16, from_core, quad16, from_plane, own, own16, from_z, full,
+    counts, x_ref, g_ref, gain_ref, shift_ref, ws, wt, line, padded, edge, halo, turned, part, part16, from_core, quad16, from_plane, own16, from_z, full,
     weight_sem, halo_send, halo_recv, core_send, core_recv, plane_send, plane_recv, z_send, z_recv,
     gather_send, gather_z, gather_plane, gather_core,
 ):
@@ -346,18 +346,43 @@
 
     for i, piece in gradient_half(1 - core):
         part16[i] = piece.astype(BF16)
-    groups = plane + [chip]
+    z_order = far + [dp]
     core_copies = [
         remote(
-            part16.at[pl.ds(p * 4, 4)], from_core.at[pl.ds(p * 4, 4)],
-            core_send.at[j], core_recv.at[j], partner,
+            part16.at[pl.ds(z * 4, 4)], from_core.at[pl.ds(z * 4, 4)], core_send.at[k], core_recv.at[k], partner
         )
-        for j, p in enumerate(groups)
+        for k, z in enumerate(z_order)
     ]
     for copy in core_copies:
         copy.start()
     for i, piece in gradient_half(core):
         part[i] = piece
+
+    plane_copies = []
+    for k, z in enumerate(z_order):
+        core_copies[k].wait()
+        quad = part[pl.ds(z * 4, 4)] + from_core[pl.ds(z * 4, 4)].astype(F32)
+        part[pl.ds(z * 4, 4)] = quad
+        quad16[k] = quad.astype(BF16)
+        for j, p in enumerate(plane):
+            i = k * 3 + j
+            copy = remote(quad16.at[k, p], from_plane.at[k, j], plane_send.at[i], plane_recv.at[i], at(dp, p, core))
+            copy.start()
+            plane_copies.append(copy)
+
+    def summed_plane(k, z):
+        for j in range(3):
+            plane_copies[k * 3 + j].wait()
+        sums = from_plane[k].astype(F32)
+        return part[z * 4 + chip] + sums[0] + sums[1] + sums[2]
+
+    z_copies = []
+
+    def pass_to_z(k):
+        own16[k] = summed_plane(k, z_order[k]).astype(BF16)
+        copy = remote(own16.at[k], from_z.at[dp], z_send.at[k], z_recv.at[dp], at(z_order[k], chip, core))
+        copy.start()
+        z_copies.append(copy)
 
     loads[6].wait()
     du = jnp.zeros((ROWS, CH), F32)
@@ -366,42 +391,47 @@
     back_t = (sig_y * (1.0 + y * (1.0 - sig_y)) * du).astype(BF16).astype(F32)
     dy = jnp.where(live, (g + back_t).astype(BF16).astype(F32), 0.0)
 
-    z_order = far + [dp]
-    for j, p in enumerate(groups):
-        core_copies[j].wait()
-        quad = part[pl.ds(p * 4, 4)] + from_core[pl.ds(p * 4, 4)].astype(F32)
-        if j == 3:
-            own[...] = quad
-        else:
-            quad16[j] = quad.astype(BF16)
-    plane_copies = []
-    for k, z in enumerate(z_order):
-        for j, p in enumerate(plane):
-            i = k * 3 + j
-            copy = remote(quad16.at[j, z], from_plane.at[j, k], plane_send.at[i], plane_recv.at[i], at(dp, p, core))
-            copy.start()
-            plane_copies.append(copy)
-
-    def summed_plane(k, z):
-        for j in range(3):
-            plane_copies[k * 3 + j].wait()
-        return own[z] + from_plane[0, k].astype(F32) + from_plane[1, k].astype(F32) + from_plane[2, k].astype(F32)
-
-    z_copies = []
-
-    def pass_to_z(k):
-        own16[k] = summed_plane(k, z_order[k]).astype(BF16)
-        copy = remote(own16.at[k], from_z.at[dp], z_send.at[k], z_recv.at[dp], at(z_order[k], chip, core))
+    stage_shifts(dy, line, padded)
+
+    def taps_of(row):
+        total = jnp.zeros((ROWS, CH), F32)
+        for tap in range(3 * row, 3 * row + 3):
+            total = total + dot(
+                shifted(padded, 2 - tap % 3, 2 - tap // 3), ws[:, tap * CH : (tap + 1) * CH], 1, 0
+            )
+        return total
+
+    pass_to_z(0)
+    da = taps_of(0)
+    pass_to_z(1)
+    da = da + taps_of(1)
+    pass_to_z(2)
+    total = summed_plane(3, dp)
+    da = da + taps_of(2)
+
+    def chunk_of(core_id, z, chip_id):
+        return core_id * 16 + z * 4 + chip_id
+
+    mine = chunk_of(core, dp, chip)
+    for z in near:
+        remote(from_z.at[z], from_z.at[z], z_send.at[0], z_recv.at[z], partner).wait_recv()
+        total = total + from_z[z].astype(F32)
+    full[mine] = total.astype(BF16)
+
+    sent = []
+
+    def pass_on(chunk, device, recv_sem):
+        copy = remote(full.at[chunk], full.at[chunk], gather_send.at[len(sent)], recv_sem, device)
         copy.start()
-        z_copies.append(copy)
-
-    stage_shifts(dy, line, padded)
-    da = jnp.zeros((ROWS, CH), F32)
-    for tap in range(9):
-        da = da + dot(shifted(padded, 2 - tap % 3, 2 - tap // 3), ws[:, tap * CH : (tap + 1) * CH], 1, 0)
-        if tap in (4, 6, 8):
-            pass_to_z(tap // 2 - 2)
-    total = summed_plane(3, dp)
+        sent.append(copy)
+
+    def await_chunk(chunk, recv_sem):
+        remote(full.at[chunk], full.at[chunk], gather_send.at[0], recv_sem, partner).wait_recv()
+
+    for z in far:
+        pass_on(mine, at(z, chip, core), gather_z.at[dp])
+    for j, p in enumerate(plane):
+        pass_on(mine, at(dp, p, core), gather_plane.at[dp * 3 + j])
 
     dhat = da * (sig_n * (1.0 + normed * (1.0 - sig_n))) * gain
     dhat_frames = [frame_of(dhat, s) for s in range(CAP)]
@@ -417,38 +447,15 @@
     )
     out_ref[...] = jnp.where(live, dy + dx, 0.0).astype(BF16)
 
-    first = core * 16 + chip * 4
-    mine = first + dp
     for z in near:
-        remote(from_z.at[z], from_z.at[z], z_send.at[0], z_recv.at[z], partner).wait_recv()
-        total = total + from_z[z].astype(F32)
-    full[mine] = total.astype(BF16)
-
-    sent = []
-
-    def pass_on(chunk, device, recv_sem):
-        copy = remote(full.at[chunk], full.at[chunk], gather_send.at[len(sent)], recv_sem, device)
-        copy.start()
-        sent.append(copy)
-
-    def await_chunk(chunk, recv_sem):
-        remote(full.at[chunk], full.at[chunk], gather_send.at[0], recv_sem, partner).wait_recv()
-
-    for z in far:
-        pass_on(mine, at(z, chip, core), gather_z.at[dp])
-    for j, p in enumerate(plane):
-        pass_on(mine, at(dp, p, core), gather_plane.at[dp * 3 + j])
-    pass_on(mine, partner, gather_core.at[dp * 4 + 3])
-    for z in near:
-        await_chunk(first + z, gather_z.at[z])
+        chunk = chunk_of(core, z, chip)
+        await_chunk(chunk, gather_z.at[z])
         for j, p in enumerate(plane):
-            pass_on(first + z, at(dp, p, core), gather_plane.at[z * 3 + j])
-        pass_on(first + z, partner, gather_core.at[z * 4 + 3])
+            pass_on(chunk, at(dp, p, core), gather_plane.at[z * 3 + j])
     for z in [dp] + near:
         for j, p in enumerate(plane):
-            chunk = core * 16 + p * 4 + z
-            await_chunk(chunk, gather_plane.at[z * 3 + j])
-            pass_on(chunk, partner, gather_core.at[z * 4 + j])
+            await_chunk(chunk_of(core, z, p), gather_plane.at[z * 3 + j])
+        pass_on(pl.ds(chunk_of(core, z, 0), 4), partner, gather_core.at[z])
 
     scale = 1.0 / math.sqrt(4 * 2 * 8 * PIX)
 
@@ -462,8 +469,7 @@
 
     put(core)
     for z in [dp] + near:
-        for j, p in enumerate(groups):
-            await_chunk((1 - core) * 16 + p * 4 + z, gather_core.at[z * 4 + j])
+        await_chunk(pl.ds(chunk_of(1 - core, z, 0), 4), gather_core.at[z])
     put(1 - core)
     for copy in z_copies + sent:
         copy.wait_send()
@@ -497,14 +503,13 @@
             pltpu.VMEM((16, BLOCK, LANE), F32),
             pltpu.VMEM((16, BLOCK, LANE), BF16),
             pltpu.VMEM((16, BLOCK, LANE), BF16),
-            pltpu.VMEM((3, 4, BLOCK, LANE), BF16),
-            pltpu.VMEM((3, 4, BLOCK, LANE), BF16),
-            pltpu.VMEM((4, BLOCK, LANE), F32),
+            pltpu.VMEM((4, 4, BLOCK, LANE), BF16),
+            pltpu.VMEM((4, 3, BLOCK, LANE), BF16),
             pltpu.VMEM((3, BLOCK, LANE), BF16),
             pltpu.VMEM((4, BLOCK, LANE), BF16),
             pltpu.VMEM((CHUNKS, BLOCK, LANE), BF16),
             dma((7,)), dma((2,)), dma((2,)), dma((4,)), dma((4,)), dma((12,)), dma((12,)), dma((3,)), dma((4,)),
-            dma((31,)), dma((4,)), dma((12,)), dma((16,)),
+            dma((19,)), dma((4,)), dma((12,)), dma((4,)),
         ],
         compiler_params=pltpu.CompilerParams(
             collective_id=0, has_side_effects=True, vmem_limit_bytes=60 * 1024 * 1024

time: 31.9 us -> 31.9 us (level)
  no operation moved by 1% of the time
where the time goes in v5:
time: 31.9 us; the launch traced here: 31.8 us
  Pallas kernels  29.4 us (92%)
  local copies, waits for them, and re-layouts  1.72 us (5%)
  between operations  0.64 us (2%)
    pallas_call x1, Pallas kernels, fused_shards(): pl.pallas_call(fused_kernel, out_shape=(pltpu.VMEM((ROWS, CH), BF16), plt...  29.4 us
    unnamed x2, local copies, waits for them, and re-layouts  1.72 us

profile of v5, /device:TPU:0, one launch (start us, length us, event | category | flops | bytes accessed | tf_op | source)
XLA Modules:
  0.0 31.8 jit_solution(12360066362875274627)
XLA Ops:
  0.6 29.4 %shard_map.86 = (bf16[192,320]{1,0:T(8,128)(2,1)S(1)}, f32[320,960]{1,0:T(8,128)S(1)}) custom-call(s32[1,8]{1,0:T(1,128)} %counts_hbm.1, bf16[192,320]{1,0:T(8,128)(2,1)} %bitcast.10, bf16[192,320]{1,0:T(8,128)(2,1)} %bitcast.11, f32[320]{0:T(512)} %gain_hbm.1, f32[320]{0:T(512)} %shift_hbm.1, bf16[320,2880]{1,0:T(8,128)(2,1)} %bitcast.8, ...), custom_call_target="tpu_custom_call" | custom-call | tf_op jit(solution)/shard_map/pallas_call | solution.py:482
  30.0 0.7 %copy.11 = bf16[1,3,8,8,320]{4,3,2,1,0:T(8,128)(2,1)} copy(bf16[1,3,8,8,320]{4,3,2,1,0:T(8,128)(2,1)S(1)} %bitcast.7) | data formatting | bytes 245760
  30.7 1.1 %copy.12 = f32[960,320]{0,1:T(8,128)} copy(f32[960,320]{0,1:T(8,128)S(1)} %bitcast.6) | data formatting | bytes 2457600

commit v6 on v5

--- a/solution.py
+++ b/solution.py
@@ -233,7 +233,7 @@
 
 def fused_kernel(
     counts_hbm, x_hbm, g_hbm, gain_hbm, shift_hbm, ws_hbm, wt_hbm, out_ref, grad_ref,
-    counts, x_ref, g_ref, gain_ref, shift_ref, ws, wt, line, padded, edge, halo, turned, part, part16, from_core, quad16, from_plane, own16, from_z, full,
+    counts, x_ref, g_ref, gain_ref, shift_ref, ws, wt, line, padded, edge, halo, turned, part, part16, from_core, quad16, from_first, second16, from_second, own16, from_z, full,
     weight_sem, halo_send, halo_recv, core_send, core_recv, plane_send, plane_recv, z_send, z_recv,
     gather_send, gather_z, gather_plane, gather_core,
 ):
@@ -358,23 +358,35 @@
     for i, piece in gradient_half(core):
         part[i] = piece
 
-    plane_copies = []
+    routes = [(plane[k % 2], plane[1 - k % 2]) for k in range(4)]
+    first_copies, second_copies = [], []
     for k, z in enumerate(z_order):
         core_copies[k].wait()
-        quad = part[pl.ds(z * 4, 4)] + from_core[pl.ds(z * 4, 4)].astype(F32)
-        part[pl.ds(z * 4, 4)] = quad
-        quad16[k] = quad.astype(BF16)
-        for j, p in enumerate(plane):
-            i = k * 3 + j
-            copy = remote(quad16.at[k, p], from_plane.at[k, j], plane_send.at[i], plane_recv.at[i], at(dp, p, core))
-            copy.start()
-            plane_copies.append(copy)
+        part[pl.ds(z * 4, 4)] = part[pl.ds(z * 4, 4)] + from_core[pl.ds(z * 4, 4)].astype(F32)
+        quad16[k, 0] = part[z * 4 + routes[k][0]].astype(BF16)
+        quad16[k, 1] = part[z * 4 + plane[2]].astype(BF16)
+        copy = remote(
+            quad16.at[k], from_first.at[k], plane_send.at[k], plane_recv.at[k], at(dp, routes[k][0], core)
+        )
+        copy.start()
+        first_copies.append(copy)
+
+    def second_step(k):
+        first_copies[k].wait()
+        second16[k] = (part[z_order[k] * 4 + routes[k][1]] + from_first[k, 1].astype(F32)).astype(BF16)
+        copy = remote(
+            second16.at[k], from_second.at[k], plane_send.at[4 + k], plane_recv.at[4 + k],
+            at(dp, routes[k][1], core),
+        )
+        copy.start()
+        second_copies.append(copy)
 
     def summed_plane(k, z):
-        for j in range(3):
-            plane_copies[k * 3 + j].wait()
-        sums = from_plane[k].astype(F32)
-        return part[z * 4 + chip] + sums[0] + sums[1] + sums[2]
+        second_copies[k].wait()
+        return part[z * 4 + chip] + from_first[k, 0].astype(F32) + from_second[k].astype(F32)
+
+    second_step(0)
+    second_step(1)
 
     z_copies = []
 
@@ -392,6 +404,8 @@
     dy = jnp.where(live, (g + back_t).astype(BF16).astype(F32), 0.0)
 
     stage_shifts(dy, line, padded)
+    second_step(2)
+    second_step(3)
 
     def taps_of(row):
         total = jnp.zeros((ROWS, CH), F32)
@@ -430,7 +444,7 @@
 
     for z in far:
         pass_on(mine, at(z, chip, core), gather_z.at[dp])
-    for j, p in enumerate(plane):
+    for j, p in enumerate(plane[:2]):
         pass_on(mine, at(dp, p, core), gather_plane.at[dp * 3 + j])
 
     dhat = da * (sig_n * (1.0 + normed * (1.0 - sig_n))) * gain
@@ -450,11 +464,14 @@
     for z in near:
         chunk = chunk_of(core, z, chip)
         await_chunk(chunk, gather_z.at[z])
-        for j, p in enumerate(plane):
+        for j, p in enumerate(plane[:2]):
             pass_on(chunk, at(dp, p, core), gather_plane.at[z * 3 + j])
+    for k, z in enumerate([dp] + near):
+        for j, p in enumerate(plane[:2]):
+            await_chunk(chunk_of(core, z, p), gather_plane.at[z * 3 + j])
+        pass_on(chunk_of(core, z, plane[k % 2]), at(dp, plane[1 - k % 2], core), gather_plane.at[z * 3 + 2])
     for z in [dp] + near:
-        for j, p in enumerate(plane):
-            await_chunk(chunk_of(core, z, p), gather_plane.at[z * 3 + j])
+        await_chunk(chunk_of(core, z, plane[2]), gather_plane.at[z * 3 + 2])
         pass_on(pl.ds(chunk_of(core, z, 0), 4), partner, gather_core.at[z])
 
     scale = 1.0 / math.sqrt(4 * 2 * 8 * PIX)
@@ -503,12 +520,14 @@
             pltpu.VMEM((16, BLOCK, LANE), F32),
             pltpu.VMEM((16, BLOCK, LANE), BF16),
             pltpu.VMEM((16, BLOCK, LANE), BF16),
-            pltpu.VMEM((4, 4, BLOCK, LANE), BF16),
-            pltpu.VMEM((4, 3, BLOCK, LANE), BF16),
+            pltpu.VMEM((4, 2, BLOCK, LANE), BF16),
+            pltpu.VMEM((4, 2, BLOCK, LANE), BF16),
+            pltpu.VMEM((4, BLOCK, LANE), BF16),
+            pltpu.VMEM((4, BLOCK, LANE), BF16),
             pltpu.VMEM((3, BLOCK, LANE), BF16),
             pltpu.VMEM((4, BLOCK, LANE), BF16),
             pltpu.VMEM((CHUNKS, BLOCK, LANE), BF16),
-            dma((7,)), dma((2,)), dma((2,)), dma((4,)), dma((4,)), dma((12,)), dma((12,)), dma((3,)), dma((4,)),
+            dma((7,)), dma((2,)), dma((2,)), dma((4,)), dma((4,)), dma((8,)), dma((8,)), dma((3,)), dma((4,)),
             dma((19,)), dma((4,)), dma((12,)), dma((4,)),
         ],
         compiler_params=pltpu.CompilerParams(

time: 31.9 us -> 35.7 us (1.12)
  Pallas kernels: 29.4 us -> 33.2 us
    pallas_call x1, Pallas kernels: 29.4 us -> 33.2 us  [fused_shards(): pl.pallas_call(fused_kernel, out_shape=(pltpu.VMEM((ROWS, CH), BF16), plt...]
where the time goes in v6:
time: 35.7 us; the launch traced here: 35.5 us
  Pallas kernels  33.2 us (93%)
  local copies, waits for them, and re-layouts  1.72 us (5%)
  between operations  0.64 us (2%)
    pallas_call x1, Pallas kernels, fused_shards(): pl.pallas_call(fused_kernel, out_shape=(pltpu.VMEM((ROWS, CH), BF16), plt...  33.2 us
    unnamed x2, local copies, waits for them, and re-layouts  1.72 us

profile of v6, /device:TPU:0, one launch (start us, length us, event | category | flops | bytes accessed | tf_op | source)
XLA Modules:
  0.0 35.5 jit_solution(3792611402868705074)
XLA Ops:
  0.6 33.2 %shard_map.86 = (bf16[192,320]{1,0:T(8,128)(2,1)S(1)}, f32[320,960]{1,0:T(8,128)S(1)}) custom-call(s32[1,8]{1,0:T(1,128)} %counts_hbm.1, bf16[192,320]{1,0:T(8,128)(2,1)} %bitcast.10, bf16[192,320]{1,0:T(8,128)(2,1)} %bitcast.11, f32[320]{0:T(512)} %gain_hbm.1, f32[320]{0:T(512)} %shift_hbm.1, bf16[320,2880]{1,0:T(8,128)(2,1)} %bitcast.8, ...), custom_call_target="tpu_custom_call" | custom-call | tf_op jit(solution)/shard_map/pallas_call | solution.py:499
  33.8 0.7 %copy.11 = bf16[1,3,8,8,320]{4,3,2,1,0:T(8,128)(2,1)} copy(bf16[1,3,8,8,320]{4,3,2,1,0:T(8,128)(2,1)S(1)} %bitcast.7) | data formatting | bytes 245760
  34.5 1.1 %copy.12 = f32[960,320]{0,1:T(8,128)} copy(f32[960,320]{0,1:T(8,128)S(1)} %bitcast.6) | data formatting | bytes 2457600

commit v7 on v3

--- a/solution.py
+++ b/solution.py
@@ -466,6 +466,17 @@
     put(1 - core)
     for copy in z_copies + sent:
         copy.wait_send()
+
+
+def place_kernel(out_from, grad_from, out_to, grad_to, sems):
+    copies = [
+        pltpu.make_async_copy(grad_from, grad_to, sems.at[0]),
+        pltpu.make_async_copy(out_from, out_to, sems.at[1]),
+    ]
+    for copy in copies:
+        copy.start()
+    for copy in copies:
+        copy.wait()
 
 
 def fused_shards(frames_in, cotangent, counts, norm_gain, norm_shift, spatial_weight, temporal_weight):
@@ -516,6 +527,14 @@
         spatial_weight.T,
         temporal_weight.T,
     )
+    anywhere = pl.BlockSpec(memory_space=pl.ANY)
+    out, grad = pl.pallas_call(
+        place_kernel,
+        out_shape=(jax.ShapeDtypeStruct(out.shape, BF16), jax.ShapeDtypeStruct(grad.shape, F32)),
+        in_specs=[anywhere, anywhere],
+        out_specs=(anywhere, anywhere),
+        scratch_shapes=[dma((2,))],
+    )(out, grad)
     return out.reshape(frames_in.shape), grad.T
 
 

time: 31.5 us -> 76.8 us (2.44)
  Pallas kernels: 29 us -> 74.3 us
    pallas_call x0 -> x1, Pallas kernels: none -> 45.3 us  [fused_shards(): pl.pallas_call(place_kernel, out_shape=(jax.ShapeDtypeStruct(out.shape, B...]
    unnamed x2 -> x4, local copies, waits for them, and re-layouts: 1.72 us -> 1.72 us
where the time goes in v7:
time: 76.8 us; the launch traced here: 76.7 us
  Pallas kernels  74.3 us (97%)
  local copies, waits for them, and re-layouts  1.72 us (2%)
    pallas_call x1, Pallas kernels, fused_shards(): pl.pallas_call(place_kernel, out_shape=(jax.ShapeDtypeStruct(out.shape, B...  45.3 us
    pallas_call x1, Pallas kernels, fused_shards(): pl.pallas_call(fused_kernel, out_shape=(pltpu.VMEM((ROWS, CH), BF16), plt...  29 us
    unnamed x4, local copies, waits for them, and re-layouts  1.72 us

profile of v7, /device:TPU:0, one launch (start us, length us, event | category | flops | bytes accessed | tf_op | source)
XLA Modules:
  0.0 76.7 jit_solution(1791608754879966651)
XLA Ops:
  0.6 29.0 %shard_map.86 = (bf16[192,320]{1,0:T(8,128)(2,1)S(1)}, f32[320,960]{1,0:T(8,128)S(1)}) custom-call(s32[1,8]{1,0:T(1,128)} %counts_hbm.1, bf16[192,320]{1,0:T(8,128)(2,1)} %bitcast.8, bf16[192,320]{1,0:T(8,128)(2,1)} %bitcast.9, f32[320]{0:T(512)} %gain_hbm.1, f32[320]{0:T(512)} %shift_hbm.1, bf16[320,2880]{1,0:T(8,128)(2,1)} %bitcast.6, bf16[320,960]{1,0:T(8,128)(2,1)} %bitcast.7), custom_call_target="tpu_custom_call" | custom-call | tf_op jit(solution)/shard_map/pallas_call | solution.py:486
  29.6 0.0 copy-start
  29.6 1.0 %copy-done = f32[320,960]{1,0:T(8,128)} copy-done((f32[320,960]{1,0:T(8,128)}, f32[320,960]{1,0:T(8,128)S(1)}, u32[]{:S(2)}) %copy-start) | copy-done | bytes 1228824
  30.7 0.0 copy-start.1
  30.7 0.7 copy-done.1
  31.4 45.3 %shard_map.87 = (bf16[192,320]{1,0:T(8,128)(2,1)}, f32[320,960]{1,0:T(8,128)}) custom-call(bf16[192,320]{1,0:T(8,128)(2,1)} %copy-done.1, f32[320,960]{1,0:T(8,128)} %copy-done), custom_call_target="tpu_custom_call" | custom-call | tf_op jit(solution)/shard_map/pallas_call | solution.py:531
Async XLA Ops:
  29.6 1.1 %copy-start = (f32[320,960]{1,0:T(8,128)}, f32[320,960]{1,0:T(8,128)S(1)}, u32[]{:S(2)}) copy-start(f32[320,960]{1,0:T(8,128)S(1)} %get-tuple-element.7.grad_from) | copy-start | bytes 3686404
  30.7 0.7 copy-start.1

commit v8 on v7

--- a/solution.py
+++ b/solution.py
@@ -531,9 +531,10 @@
     out, grad = pl.pallas_call(
         place_kernel,
         out_shape=(jax.ShapeDtypeStruct(out.shape, BF16), jax.ShapeDtypeStruct(grad.shape, F32)),
-        in_specs=[anywhere, anywhere],
+        in_specs=[vmem, vmem],
         out_specs=(anywhere, anywhere),
         scratch_shapes=[dma((2,))],
+        compiler_params=pltpu.CompilerParams(vmem_limit_bytes=4 * 1024 * 1024),
     )(out, grad)
     return out.reshape(frames_in.shape), grad.T
 

time: 76.8 us -> 30.9 us (0.40)
  Pallas kernels: 74.3 us -> 30.1 us
  local copies, waits for them, and re-layouts: 1.72 us -> 0 us
    pallas_call x1, Pallas kernels: 45.3 us -> 1.11 us  [fused_shards(): pl.pallas_call(place_kernel, out_shape=(jax.ShapeDtypeStruct(out.shape, B...]
    unnamed x4 -> x0, local copies, waits for them, and re-layouts: 1.72 us -> none
where the time goes in v8:
time: 30.9 us; the launch traced here: 30.7 us
  Pallas kernels  30.1 us (97%)
  between operations  0.64 us (2%)
    pallas_call x1, Pallas kernels, fused_shards(): pl.pallas_call(fused_kernel, out_shape=(pltpu.VMEM((ROWS, CH), BF16), plt...  29 us
    pallas_call x1, Pallas kernels, fused_shards(): pl.pallas_call(place_kernel, out_shape=(jax.ShapeDtypeStruct(out.shape, B...  1.11 us

profile of v8, /device:TPU:0, one launch (start us, length us, event | category | flops | bytes accessed | tf_op | source)
XLA Modules:
  0.0 30.7 jit_solution(17709712117153564865)
XLA Ops:
  0.6 29.0 %shard_map.86 = (bf16[192,320]{1,0:T(8,128)(2,1)S(1)}, f32[320,960]{1,0:T(8,128)S(1)}) custom-call(s32[1,8]{1,0:T(1,128)} %counts_hbm.1, bf16[192,320]{1,0:T(8,128)(2,1)} %bitcast.8, bf16[192,320]{1,0:T(8,128)(2,1)} %bitcast.9, f32[320]{0:T(512)} %gain_hbm.1, f32[320]{0:T(512)} %shift_hbm.1, bf16[320,2880]{1,0:T(8,128)(2,1)} %bitcast.6, bf16[320,960]{1,0:T(8,128)(2,1)} %bitcast.7), custom_call_target="tpu_custom_call" | custom-call | tf_op jit(solution)/shard_map/pallas_call | solution.py:486
  29.6 1.1 %shard_map.87 = (bf16[192,320]{1,0:T(8,128)(2,1)}, f32[320,960]{1,0:T(8,128)}) custom-call(bf16[192,320]{1,0:T(8,128)(2,1)S(1)} %get-tuple-element.6.out_from, f32[320,960]{1,0:T(8,128)S(1)} %get-tuple-element.7.grad_from), custom_call_target="tpu_custom_call" | custom-call | tf_op jit(solution)/shard_map/pallas_call | solution.py:531
